TPU v7x, 256 devices: a whole 4x4x8 slice. The times are simulated.
256 devices in a mesh: blk: 64 (over z, y, core), lon: 4 (over x).
Axes of the slice: x: 4, y: 4, z: 8, core: 2. Of those that a mesh axis runs over, the one named last changes fastest.
Arguments:
- spectra: float32 [64, 4, 2, 2, 2, 16384], P(None, 'lon', None, None, None, 'blk'), may hold values from -0.046875 to 0.046875
- source_tiles: int32 [64, 32, 2], P('blk', 'lon'), may hold values from 0 to 63, as said below
- tap_shift: int32 [64, 32, 2], P('blk', 'lon'), may hold values from -448 to 448
- kernels: float32 [64, 32, 2, 128], P('blk', 'lon'), may hold values from -0.375 to 0.375
Outputs:
- unlensed: float32 [512, 2, 32768], P('blk', None, 'lon')
- lensed: float32 [512, 2, 32768], P('blk', None, 'lon')
Inputs may be any that keep to these rules, and one draw needn't show every extreme that they name: `source_tiles`: each source tile lies at most one cycle tile away from its reader tile's cycle tile.
All inputs are finite; a program needn't handle non-finite values.
Results may differ from a plain program's by a relative error of at most 0.0003.
Values sent between devices are 32-bit elements; how exact they have to be, the bound alone decides.
A program may use at most 128 MiB of HBM per device.

v0:
```python
import math

import jax
import jax.numpy as jnp
from jax import lax
from jax.sharding import PartitionSpec as P

CYCLE_PIXELS = 32768
ORDER_RADIX = 128
TAPS = 128
MAXSHIFT = 448
TROWS = 8
PTILE = 1024


HIGHEST = lax.Precision.HIGHEST


def padded(block, sides, width, periodic):
    for axis, dim in sides:
        count = lax.axis_size(axis)
        forward = [(i, i + 1) for i in range(count - 1)]
        if periodic:
            forward.append((count - 1, 0))
        backward = [(target, source) for source, target in forward]
        low = lax.ppermute(
            lax.slice_in_dim(block, block.shape[dim] - width, None, axis=dim), axis, forward
        )
        high = lax.ppermute(lax.slice_in_dim(block, 0, width, axis=dim), axis, backward)
        block = jnp.concatenate([low, block, high], axis=dim)
    return block


def phase_angles_grid(row_count, col_count, period, col_start):
    row_index = jnp.arange(row_count, dtype=jnp.int32)[:, None]
    col_index = (jnp.arange(col_count, dtype=jnp.int32) + col_start)[None, :]
    turns = row_index * col_index % period
    phase = turns.astype(jnp.float32) * jnp.float32(2.0 * math.pi / period)
    return (jnp.cos(phase), jnp.sin(phase))


def synthesize_cycles(harmonic_spectrum, upper_order_start, upper_order_count):
    number_cycles = harmonic_spectrum.shape[0]
    upper_order_digit = harmonic_spectrum.shape[3] // ORDER_RADIX
    lower_pixel_digits = CYCLE_PIXELS // ORDER_RADIX
    spectrum_matrix = harmonic_spectrum.reshape(number_cycles, 2, 2, upper_order_digit, ORDER_RADIX)
    real_part = spectrum_matrix[:, :, 0]
    imag_part = spectrum_matrix[:, :, 1]
    cos_first, sin_first = phase_angles_grid(
        upper_order_digit, lower_pixel_digits, lower_pixel_digits, jnp.int32(0)
    )
    first_real = jnp.einsum("rcab,aj->rcbj", real_part, cos_first, precision=HIGHEST) - jnp.einsum(
        "rcab,aj->rcbj", imag_part, sin_first, precision=HIGHEST
    )
    first_imag = jnp.einsum("rcab,aj->rcbj", real_part, sin_first, precision=HIGHEST) + jnp.einsum(
        "rcab,aj->rcbj", imag_part, cos_first, precision=HIGHEST
    )
    cosine_rotation, sine_rotation = phase_angles_grid(
        ORDER_RADIX, lower_pixel_digits, CYCLE_PIXELS, jnp.int32(0)
    )
    twist_real = first_real * cosine_rotation - first_imag * sine_rotation
    twist_imag = first_real * sine_rotation + first_imag * cosine_rotation
    cosine_final, sine_final = phase_angles_grid(
        ORDER_RADIX, upper_order_count, ORDER_RADIX, upper_order_start
    )
    pixels = jnp.einsum("rcbj,bk->rckj", twist_real, cosine_final, precision=HIGHEST) - jnp.einsum(
        "rcbj,bk->rckj", twist_imag, sine_final, precision=HIGHEST
    )
    return pixels.reshape(number_cycles, 2, upper_order_count * lower_pixel_digits)


def tile_values(grid, row_start, col_start, taps):
    width = taps.shape[0]
    block_start = col_start // width
    offset = col_start - block_start * width
    count = PTILE // width
    window = lax.dynamic_slice(
        grid, (row_start, jnp.int32(0), block_start, jnp.int32(0)), (TROWS, 2, count + 2, width)
    )
    triple = jnp.concatenate([window[:, :, :-2], window[:, :, 1:-1], window[:, :, 2:]], axis=3)
    spread = jnp.concatenate(
        [jnp.zeros((width,), taps.dtype), taps, jnp.zeros((2 * width + 1,), taps.dtype)]
    )
    placed = lax.dynamic_slice(spread, (jnp.int32(width) - offset,), (3 * width + 1,))
    toeplitz = jnp.tile(placed, width)[: 3 * width * width].reshape(width, 3 * width)
    result = jnp.einsum("rcbu,qu->rcbq", triple, toeplitz, precision=HIGHEST)
    return result.reshape(TROWS, 2, PTILE)


def lens_band(extended, sources, shifts, kernels, tile_base, halo_cols):
    tile_rows, tile_cols, source_count = sources.shape
    width = kernels.shape[3]
    padded_band = jnp.concatenate(
        [extended, jnp.zeros((extended.shape[0], 2, width), extended.dtype)], axis=2
    )
    grid = padded_band.reshape(extended.shape[0], 2, padded_band.shape[2] // width, width)
    row_start = (sources - tile_base) * TROWS + TROWS
    col_base = (jnp.arange(tile_cols, dtype=jnp.int32) * PTILE)[None, :, None]
    col_start = col_base + shifts - TAPS // 2 + halo_cols
    item_count = tile_rows * tile_cols * source_count
    values = jax.vmap(tile_values, in_axes=(None, 0, 0, 0))(
        grid,
        row_start.reshape(item_count),
        col_start.reshape(item_count),
        kernels.reshape(item_count, width),
    )
    values = values.reshape(tile_rows, tile_cols, source_count, TROWS, 2, PTILE).sum(axis=2)
    values = values.transpose(0, 2, 3, 1, 4)
    return values.reshape(tile_rows * TROWS, 2, tile_cols * PTILE)


def shards(spectra, source_tiles, tap_shift, kernels):
    arrived = lax.all_to_all(spectra, "blk", split_axis=0, concat_axis=5, tiled=True)
    own_cycles = arrived.shape[2]
    mine = arrived.reshape(own_cycles, 2, 2, arrived.shape[5])
    longitude_count = lax.axis_size("lon")
    lon_place = lax.axis_index("lon")
    device_portion = ORDER_RADIX // longitude_count
    unlensed = synthesize_cycles(
        lax.all_gather(mine, "lon", axis=0, tiled=True), lon_place * device_portion, device_portion
    )
    halo_cols = MAXSHIFT + TAPS // 2
    widened = padded(unlensed, (("lon", 2),), halo_cols, True)
    extended = padded(widened, (("blk", 0),), TROWS, False)
    tile_base = lax.axis_index("blk") * source_tiles.shape[0]
    lensed = lens_band(extended, source_tiles, tap_shift, kernels, tile_base, halo_cols)
    return (unlensed, lensed)


def solution(mesh):
    placed = (
        P(None, "lon", None, None, None, "blk"),
        P("blk", "lon", None),
        P("blk", "lon", None),
        P("blk", "lon", None, None),
    )
    return jax.shard_map(
        shards,
        mesh=mesh,
        in_specs=placed,
        out_specs=(P("blk", None, "lon"), P("blk", None, "lon")),
        check_vma=False,
    )
```

profile of v0, /device:TPU:1, one launch (start us, length us, event | category | flops | bytes accessed | tf_op | source)
XLA Modules:
  0.0 164.0 jit_solution(1708311853444206359)
XLA Ops:
  7.2 30.9 %all_to_all.15 = f32[64,1,2,2,2,256]{5,4,3,2,1,0:T(2,128)S(1)} all-to-all(f32[64,1,2,2,2,256]{5,4,3,2,1,0:T(2,128)} %param.4), channel_id=1, replica_groups=mesh['blk'=64,'lon'=4] {'blk'}, dimensions={0} | all-to-all | bytes 1048576 | tf_op jit(solution)/shard_map/all_to_all | solution.py:113
  40.3 29.1 %all-gather.2.cloned.1.call-done = f32[8,2,2,16384]{3,2,1,0:T(2,128)} async-done(((f32[2,2,2,16384]{3,2,1,0:T(2,128)}), f32[8,2,2,16384]{3,2,1,0:T(2,128)}) %all-gather.2.cloned.1.call-update) | async-done | bytes 2097168 | tf_op jit(solution)/shard_map/all_gather | solution.py:120
  69.3 3.2 %reshape.270 = f32[8,2,2,128,128]{4,3,2,1,0:T(8,128)S(1)} reshape(f32[8,2,2,16384]{3,2,1,0:T(2,128)} %all-gather.2.cloned.1.call-done) | data formatting | bytes 4194304 | tf_op jit(solution)/shard_map/reshape | solution.py:46
  72.6 2.3 %fusion.24 = f32[256,8,2,128]{3,0,2,1:T(8,128)S(1)} fusion(f32[8,2,2,128,128]{4,3,2,1,0:T(8,128)S(1)} %reshape.270), kind=kOutput, calls=%fused_computation.30 | convolution fusion | flops 805765120 | bytes 3145728 | tf_op jit(solution)/shard_map/rcab,aj->rcbj/dot_general | solution.py:55
  74.9 2.3 %fusion.25 = f32[256,8,2,128]{3,0,2,1:T(8,128)S(1)} fusion(f32[8,2,2,128,128]{4,3,2,1,0:T(8,128)S(1)} %reshape.270), kind=kOutput, calls=%fused_computation.31 | convolution fusion | flops 805765120 | bytes 3145728 | tf_op jit(solution)/shard_map/rcab,aj->rcbj/dot_general | solution.py:52
  77.2 2.3 %convolution_add_fusion = f32[256,8,2,128]{3,0,2,1:T(8,128)S(1)} fusion(f32[256,8,2,128]{3,0,2,1:T(8,128)S(1)} %fusion.24, f32[8,2,2,128,128]{4,3,2,1,0:T(8,128)S(1)} %reshape.270), kind=kOutput, calls=%fused_computation.20 | convolution fusion | flops 806289408 | bytes 5242880 | tf_op jit(solution)/shard_map/rcab,aj->rcbj/dot_general | solution.py:55
  79.5 2.3 %convolution_subtract_fusion = f32[256,8,2,128]{3,0,2,1:T(8,128)S(1)} fusion(f32[256,8,2,128]{3,0,2,1:T(8,128)S(1)} %fusion.25, f32[8,2,2,128,128]{4,3,2,1,0:T(8,128)S(1)} %reshape.270), kind=kOutput, calls=%fused_computation.21 | convolution fusion | flops 806289408 | bytes 5242880 | tf_op jit(solution)/shard_map/rcab,aj->rcbj/dot_general | solution.py:52
  81.8 2.5 %fusion.8 = f32[32,8,2,256]{3,0,2,1:T(8,128)S(1)} fusion(f32[256,8,2,128]{3,0,2,1:T(8,128)S(1)} %convolution_add_fusion, f32[256,8,2,128]{3,0,2,1:T(8,128)S(1)} %convolution_subtract_fusion, f32[128,256]{0,1:T(8,128)S(1)} %get-tuple-element.29, f32[128,256]{0,1:T(8,128)S(1)} %get-tuple-element.30, s32[32]{0:T(128)S(1)} %iota_add_fusion), kind=kOutput, calls=%fused_computation.12 | convolution fusion | flops 202956800 | bytes 4980864 | tf_op jit(solution)/shard_map/rcbj,bk->rckj/dot_general | solution.py:66
  84.2 2.5 %fusion.17 = f32[8,2,32,256]{3,2,1,0:T(8,128)S(1)} fusion(f32[32,8,2,256]{3,0,2,1:T(8,128)S(1)} %fusion.8, f32[256,8,2,128]{3,0,2,1:T(8,128)S(1)} %convolution_add_fusion, f32[256,8,2,128]{3,0,2,1:T(8,128)S(1)} %convolution_subtract_fusion, f32[128,256]{0,1:T(8,128)S(1)} %get-tuple-element.29, f32[128,256]{0,1:T(8,128)S(1)} %get-tuple-element.30, ...), kind=kOutput, calls=%fused_computation.23 | convolution fusion | flops 203087872 | bytes 5505152 | tf_op jit(solution)/shard_map/rcbj,bk->rckj/dot_general | solution.py:66
  87.7 2.5 %collective-permute-start.1 = (f32[8,2,512]{2,1,0:T(2,128)S(1)}, f32[8,2,512]{2,1,0:T(2,128)S(1)}, u32[]{:S(2)}, u32[]{:S(2)}) collective-permute-start(f32[8,2,512]{2,1,0:T(2,128)S(1)} %get-tuple-element.27), channel_id=1, source_target_pairs={{1,0},{2,1},{3,2},{0,3},{5,4},{6,5},{7,6},{4,7},{9,8},{10,9},{11,1... | collective-permute-start | bytes 98312 | tf_op jit(solution)/shard_map/ppermute | solution.py:29
  93.5 3.7 %collective-permute-start.3 = (f32[8,2,9216]{2,1,0:T(2,128)}, f32[8,2,9216]{2,1,0:T(2,128)}, u32[]{:S(2)}, u32[]{:S(2)}) collective-permute-start(f32[8,2,9216]{2,1,0:T(2,128)} %constant_dynamic-update-slice_fusion), channel_id=1, source_target_pairs={{4,0},{8,4},{12,8},{16,12},{20,16},{24,20},{28,24},{32,28},{36,32}... | collective-permute-start | bytes 1769480 | tf_op jit(solution)/shard_map/ppermute | solution.py:29
  97.3 3.0 %collective-permute-start.2 = (f32[8,2,9216]{2,1,0:T(2,128)}, f32[8,2,9216]{2,1,0:T(2,128)}, u32[]{:S(2)}, u32[]{:S(2)}) collective-permute-start(f32[8,2,9216]{2,1,0:T(2,128)} %constant_dynamic-update-slice_fusion), channel_id=1, source_target_pairs={{0,4},{4,8},{8,12},{12,16},{16,20},{20,24},{24,28},{28,32},{32,36}... | collective-permute-start | bytes 1769480 | tf_op jit(solution)/shard_map/ppermute | solution.py:26
  100.3 32.8 %while.1 = (s32[]{:T(128)}, f32[16,513]{1,0:T(8,128)S(1)}, s32[16,2]{0,1:T(2,128)S(1)}, f32[16,385]{1,0:T(8,128)S(1)}, s32[]{:T(128)}, /*index=5*/s32[]{:T(128)}) while((s32[]{:T(128)}, f32[16,513]{1,0:T(8,128)S(1)}, s32[16,2]{0,1:T(2,128)S(1)}, f32[16,385]{1,0:T(8,128)S(1)}, s32[]{:T(128)}, /*index=5*/s32[]{:T(128)}) %tuple.29), condition=%wide.while_cond, body=%wide.while_body.sunk | while | flops 2 | bytes 6281 | solution.py:84
  100.9 1.3 dynamic-slice.7
  103.0 1.3 dynamic-slice.7
  105.0 1.3 dynamic-slice.7
  133.2 2.5 %tile.4 = f32[16,128,385]{2,1,0:T(8,128)} broadcast(f32[16,385]{1,0:T(8,128)S(1)} %get-tuple-element.9), dimensions={0,2} | broadcast | bytes 3178560 | tf_op jit(solution)/shard_map/vmap()/tile | solution.py:85
  135.7 3.6 %tile.10 = f32[16,49280]{1,0:T(8,128)S(1)} reshape(f32[16,128,385]{2,1,0:T(8,128)} %tile.4) | data formatting | bytes 6307840 | tf_op jit(solution)/shard_map/vmap()/tile | solution.py:85
  139.6 2.2 %copy.57 = f32[2,8,128,384]{3,2,1,0:T(8,128)} copy(f32[2,8,128,384]{3,1,2,0:T(8,128)S(1)} %bitcast.97) | data formatting | bytes 6291456
  141.9 2.5 %fusion.13 = f32[24,2,73,128]{3,1,2,0:T(2,128)S(1)} fusion(f32[8,2,9216]{2,1,0:T(2,128)} %collective-permute-done.3, f32[8,2,9216]{2,1,0:T(2,128)} %constant_dynamic-update-slice_fusion, f32[8,2,9216]{2,1,0:T(2,128)} %collective-permute-done.2), kind=kLoop, calls=%fused_computation.18 | loop fusion | flops 2691072 | bytes 3563520 | tf_op jit(solution)/shard_map/reshape | solution.py:96
  144.4 2.0 %gather_fusion = f32[16,8,2,10,128]{4,2,3,1,0:T(2,128)S(1)} fusion(f32[24,2,73,128]{3,1,2,0:T(2,128)S(1)} %fusion.13, s32[16]{0:T(128)S(1)} %fusion.66), kind=kCustom, calls=%fused_computation | custom fusion | bytes 2621696 | tf_op jit(solution)/shard_map/vmap()/gather | solution.py:77
  146.4 1.7 %fusion.93 = (f32[16,8,2,8,128]{4,2,3,1,0:T(2,128)S(1)}, f32[16,8,2,8,128]{4,2,3,1,0:T(2,128)S(1)}, f32[16,8,2,8,128]{4,2,3,1,0:T(2,128)S(1)}) fusion(f32[16,8,2,10,128]{4,2,3,1,0:T(2,128)S(1)} %gather_fusion), kind=kLoop, calls=%fused_computation.118 | loop fusion | bytes 6291456 | tf_op jit(solution)/shard_map/vmap()/slice | solution.py:80
  148.4 1.7 %copy-done = f32[2,8,128,384]{3,2,1,0:T(8,128)S(1)} copy-done((f32[2,8,128,384]{3,2,1,0:T(8,128)S(1)}, f32[2,8,128,384]{3,2,1,0:T(8,128)}, u32[]{:S(2)}) %copy-start) | copy-done | bytes 3145752
  150.1 4.1 %fusion = f32[16,8,2,8,128]{4,3,2,1,0:T(8,128)S(1)} fusion(f32[16,8,2,8,128]{4,3,2,1,0:T(8,128)S(1)} %copy.56, f32[16,8,2,8,128]{4,3,2,1,0:T(8,128)S(1)} %copy.55, f32[16,8,2,8,128]{4,3,2,1,0:T(8,128)S(1)} %copy.54, f32[16,128,384,1,1]{2,1,0,3,4:T(8,128)S(1)} %bitcast.96), kind=kOutput, calls=%fused_computation.2 | convolution fusion | flops 1209532416 | bytes 7340032 | tf_op jit(solution)/shard_map/vmap(rcbu,qu->rcbq)/dot_general | solution.py:86
  (111 shorter events, 38.3 us)
Async XLA Ops:
  7.2 32.3 %copy-start.3 = (s32[1,8,2]{1,2,0:T(2,128)S(1)}, s32[1,8,2]{1,2,0:T(2,128)}, u32[]{:S(2)}) copy-start(s32[1,8,2]{1,2,0:T(2,128)} %param.6) | copy-start | bytes 196
  7.2 33.1 %copy-start.2 = (f32[1,8,2,128]{3,2,1,0:T(2,128)S(1)}, f32[1,8,2,128]{3,2,1,0:T(2,128)}, u32[]{:S(2)}) copy-start(f32[1,8,2,128]{3,2,1,0:T(2,128)} %param.7) | copy-start | bytes 24580
  7.2 62.2 %all-gather.2.cloned.1.call-start = ((), (), s32[]{:S(2)}) async-start(), calls=%async_computation.1 | async-start | bytes 2621440 | tf_op jit(solution)/shard_map/all_gather | solution.py:120
  86.8 46.3 %copy-start.4 = (s32[1,8,2]{1,2,0:T(2,128)S(1)}, s32[1,8,2]{1,2,0:T(2,128)}, u32[]{:S(2)}) copy-start(s32[1,8,2]{1,2,0:T(2,128)} %param.5) | copy-start | bytes 196
  87.1 46.1 %copy-start.1 = (f32[8,2,8192]{2,1,0:T(2,128)}, f32[8,2,8192]{2,1,0:T(2,128)S(1)}, u32[]{:S(2)}) copy-start(f32[8,2,8192]{2,1,0:T(2,128)S(1)} %reshape.232) | copy-start | bytes 1572868
  87.2 4.3 %collective-permute-start = (f32[8,2,512]{2,1,0:T(2,128)S(1)}, f32[8,2,512]{2,1,0:T(2,128)S(1)}, u32[]{:S(2)}, u32[]{:S(2)}) collective-permute-start(f32[8,2,512]{2,1,0:T(2,128)S(1)} %get-tuple-element.28), channel_id=1, source_target_pairs={{0,1},{1,2},{2,3},{3,0},{4,5},{5,6},{6,7},{7,4},{8,9},{9,10},{10,1... | collective-permute-start | bytes 98312 | tf_op jit(solution)/shard_map/ppermute | solution.py:26
  87.7 5.2 %collective-permute-start.1 = (f32[8,2,512]{2,1,0:T(2,128)S(1)}, f32[8,2,512]{2,1,0:T(2,128)S(1)}, u32[]{:S(2)}, u32[]{:S(2)}) collective-permute-start(f32[8,2,512]{2,1,0:T(2,128)S(1)} %get-tuple-element.27), channel_id=1, source_target_pairs={{1,0},{2,1},{3,2},{0,3},{5,4},{6,5},{7,6},{4,7},{9,8},{10,9},{11,1... | collective-permute-start | bytes 98312 | tf_op jit(solution)/shard_map/ppermute | solution.py:29
  93.5 48.3 %collective-permute-start.3 = (f32[8,2,9216]{2,1,0:T(2,128)}, f32[8,2,9216]{2,1,0:T(2,128)}, u32[]{:S(2)}, u32[]{:S(2)}) collective-permute-start(f32[8,2,9216]{2,1,0:T(2,128)} %constant_dynamic-update-slice_fusion), channel_id=1, source_target_pairs={{4,0},{8,4},{12,8},{16,12},{20,16},{24,20},{28,24},{32,28},{36,32}... | collective-permute-start | bytes 1769480 | tf_op jit(solution)/shard_map/ppermute | solution.py:29
  97.3 44.6 %collective-permute-start.2 = (f32[8,2,9216]{2,1,0:T(2,128)}, f32[8,2,9216]{2,1,0:T(2,128)}, u32[]{:S(2)}, u32[]{:S(2)}) collective-permute-start(f32[8,2,9216]{2,1,0:T(2,128)} %constant_dynamic-update-slice_fusion), channel_id=1, source_target_pairs={{0,4},{4,8},{8,12},{12,16},{16,20},{20,24},{24,28},{28,32},{32,36}... | collective-permute-start | bytes 1769480 | tf_op jit(solution)/shard_map/ppermute | solution.py:26
  148.2 1.9 %copy-start = (f32[2,8,128,384]{3,2,1,0:T(8,128)S(1)}, f32[2,8,128,384]{3,2,1,0:T(8,128)}, u32[]{:S(2)}) copy-start(f32[2,8,128,384]{3,2,1,0:T(8,128)} %copy.57) | copy-start | bytes 9437188
Sparse Core Ops, SparseCore 0:
  39.6 29.7 all-gather.1
where the time goes:
time: 165 us; the launch traced here: 164 us
  local copies, waits for them, and re-layouts  56.1 us (34%)
  blocking collectives  30.9 us (19%)
  waiting for transfers between devices  30.3 us (18%)
  matrix products  18.3 us (11%)
  between operations  14.4 us (9%)
  starting transfers between devices  9.83 us (6%)
  other arithmetic  3.96 us (2%)
    gather x64, local copies, waits for them, and re-layouts  32.4 us
    all_to_all x1, blocking collectives, shards(): lax.all_to_all(spectra, 'blk', split_axis=0, concat_axis=5, tiled=True)  30.9 us
    all_gather x1, waiting for transfers between devices, shards(): lax.all_gather(mine, 'lon', axis=0, tiled=True)  29.1 us
    unnamed x19, local copies, waits for them, and re-layouts  7.23 us
    ppermute x2, starting transfers between devices, padded(): lax.ppermute(lax.slice_in_dim(block, 0, width, axis=dim), axis, backward)  6.23 us
    another operation x2, local copies, waits for them, and re-layouts, tile_values(): jnp.tile(placed, width)[:3 * width * width].reshape(width, 3 * width)  6.11 us
    dot_general x1, matrix products, tile_values(): result = jnp.einsum('rcbu,qu->rcbq', triple, toeplitz, precision=HIGHEST)  4.13 us
    ppermute x2, starting transfers between devices, padded(): lax.ppermute(lax.slice_in_dim(block, block.shape[dim] - width, None, axis...  3.57 us
  transfers between devices with their start and end apart: 5, of which 2 were waited for; matrix products, arithmetic and copies ran while one was open for 26% of the time, Pallas kernels for 0%

commit v1 on v0

v1 whole, which is shorter than its diff:
```python
import functools
import math

import jax
import jax.numpy as jnp
import ml_dtypes
import numpy as np
from jax import lax
from jax.experimental import pallas as pl
from jax.experimental.pallas import tpu as pltpu
from jax.sharding import PartitionSpec as P

NBLK = 64
NLON = 4
MESH = pl.DeviceIdType.MESH
F32 = jnp.float32
BF16 = jnp.bfloat16

ROWS = 72


def split(values):
    high = values.astype(ml_dtypes.bfloat16)
    low = (values - high.astype(np.float64)).astype(ml_dtypes.bfloat16)
    return high, low


def tables():
    def angle(rows, cols, period):
        return 2.0 * math.pi * ((rows[:, None] * cols[None, :]) % period) / period

    i = np.arange(128)
    b = np.arange(NBLK)
    n = np.arange(256)
    first = angle(i, b, 128)
    first = np.block([[np.cos(first), -np.sin(first)], [np.sin(first), np.cos(first)]])
    high, low = split(first)
    first = np.concatenate([high, low, high], axis=1)
    turn = angle(i, n, 32768)
    pixel_rows = np.concatenate([(64 * l + np.arange(ROWS) - 4) % 256 for l in range(NLON)])
    last = angle(pixel_rows, n, 256)
    last = np.concatenate([np.cos(last), -np.sin(last)], axis=1)
    last_high, last_low = split(last)
    return (
        first,
        np.cos(turn).astype(np.float32),
        np.sin(turn).astype(np.float32),
        last_high,
        last_low,
    )


def halves(x):
    high = x.astype(BF16)
    return high, (x - high.astype(F32)).astype(BF16)


def nt(a, b):
    return lax.dot_general(a, b, (((1,), (1,)), ((), ())), preferred_element_type=F32)


def synthesize(land, first_ref, cos_ref, sin_ref, high_ref, low_ref, made):
    for k in range(2):
        for q in range(2):
            kq = 2 * k + q
            parts = []
            for ri in range(2):
                rows = [land[pl.ds(4 * kq + 2 * h + ri, NBLK, stride=16), :] for h in range(2)]
                parts.append(jnp.concatenate(rows, axis=1))
            xh, xl = halves(jnp.concatenate(parts, axis=0))
            spread = jnp.concatenate([xh, xh, xl], axis=0)
            g = jnp.dot(first_ref[...], spread, preferred_element_type=F32)
            gre, gim = g[:128], g[128:]
            cos, sin = cos_ref[...], sin_ref[...]
            hh, hl = halves(
                jnp.concatenate([gre * cos - gim * sin, gre * sin + gim * cos], axis=1)
            )
            out = nt(high_ref[...], hh) + (nt(low_ref[...], hh) + nt(high_ref[...], hl))
            for l in range(NLON):
                made[l, k, pl.ds(q, ROWS, stride=2), :] = out[ROWS * l : ROWS * (l + 1)]


def lens(blk, src_ref, shift_ref, taps_ref, ext, lensed_ref):
    q_index = lax.broadcasted_iota(jnp.int32, (128, 128), 0)
    u_index = lax.broadcasted_iota(jnp.int32, (128, 128), 1)
    lead = u_index - q_index

    def one(g, carry):
        total = None
        for k in range(2):
            which = jnp.clip(src_ref[0, g, k] - blk + 1, 0, 2)
            start = shift_ref[0, g, k] + 448
            base = jnp.clip(lax.shift_right_arithmetic(start, 7), 0, 6)
            off = start - 128 * base
            taps = jnp.broadcast_to(taps_ref[pl.ds(2 * g + k, 1), :], (8, 128))
            taps = pltpu.roll(taps, off & 127, 1)
            ring = pltpu.roll(
                jnp.broadcast_to(taps[:1], (128, 128)), 0, 1, stride=1, stride_axis=0
            )
            toep = []
            wins = []
            for i in range(3):
                at = lead + (128 * i - off)
                toep.append(jnp.where((at >= 0) & (at < 128), ring, 0.0))
                row = 2 * (8 * g + base + i)
                wins.append(
                    jnp.concatenate(
                        [ext[which, u, pl.ds(row, 16), :] for u in range(8)], axis=0
                    )
                )
            th, tl = halves(jnp.concatenate(toep, axis=1))
            wh, wl = halves(jnp.concatenate(wins, axis=1))
            part = nt(wh, th) + (nt(wl, th) + nt(wh, tl))
            total = part if total is None else total + part
        for u in range(8):
            lensed_ref[u, pl.ds(pl.multiple_of(16 * g, 16), 16), :] = total[16 * u : 16 * u + 16]
        return carry

    lax.fori_loop(0, 8, one, 0)


def kernel(
    spec_ref, src_ref, shift_ref, taps_ref, first_ref, cos_ref, sin_ref, high_ref, low_ref,
    plain_ref, lensed_ref,
    land, made, ext, own_sem, send_a, recv_a, send_b, recv_b, send_c, recv_c,
):
    blk = lax.axis_index("blk")
    lon = lax.axis_index("lon")
    up = lax.rem(blk + 1, NBLK)
    down = lax.rem(blk + NBLK - 1, NBLK)

    barrier = pltpu.get_barrier_semaphore()

    def greet(o, carry):
        pl.semaphore_signal(
            barrier, inc=1, device_id=(lax.rem(blk + o, NBLK), lon), device_id_type=MESH
        )
        return carry

    lax.fori_loop(1, NBLK, greet, 0)
    for d in range(1, NLON):
        pl.semaphore_signal(
            barrier, inc=1, device_id=(blk, lax.rem(lon + d, NLON)), device_id_type=MESH
        )
    mine = pl.ds(pl.multiple_of(16 * blk, 16), 16)
    own = pltpu.make_async_copy(spec_ref.at[blk], land.at[mine], own_sem.at[0])
    own.start()
    pl.semaphore_wait(barrier, NBLK - 1 + NLON - 1)

    def send(o, carry):
        to = lax.rem(blk + o, NBLK)
        pltpu.make_async_remote_copy(
            src_ref=spec_ref.at[to],
            dst_ref=land.at[mine],
            send_sem=send_a,
            recv_sem=recv_a,
            device_id=(to, lon),
            device_id_type=MESH,
        ).start()
        return carry

    lax.fori_loop(1, NBLK, send, 0)
    own.wait()
    others = land.at[pl.ds(0, 16 * (NBLK - 1))]
    pltpu.make_async_copy(others, others, recv_a).wait()

    synthesize(land, first_ref, cos_ref, sin_ref, high_ref, low_ref, made)

    def across(d):
        to = lax.rem(lon + d, NLON)
        return pltpu.make_async_remote_copy(
            src_ref=made.at[to],
            dst_ref=ext.at[1, pl.ds(2 * lon, 2)],
            send_sem=send_b.at[d],
            recv_sem=recv_b.at[d],
            device_id=(blk, to),
            device_id_type=MESH,
        )

    def beside(d, source, l, to, slot, side):
        return pltpu.make_async_remote_copy(
            src_ref=source,
            dst_ref=ext.at[slot, pl.ds(2 * l, 2)],
            send_sem=send_c.at[side, d],
            recv_sem=recv_c.at[side, d],
            device_id=(to, lon),
            device_id_type=MESH,
        )

    sent_b = [across(d) for d in (1, 3, 2)]
    for copy in sent_b:
        copy.start()
    sent_c = []
    for d in (0, 1, 3, 2):
        l = lax.rem(lon + NLON - d, NLON)
        if d == 0:
            source = made.at[lon]
            keep = pltpu.make_async_copy(source, ext.at[1, pl.ds(2 * lon, 2)], own_sem.at[1])
            keep.start()
        else:
            across(d).wait_recv()
            source = ext.at[1, pl.ds(2 * l, 2)]
        for to, slot, side in ((up, 0, 0), (down, 2, 1)):
            copy = beside(d, source, l, to, slot, side)
            copy.start()
            sent_c.append(copy)
    keep.wait()
    plain_ref[...] = ext[1, :, 8:136, :]
    for copy in sent_c:
        copy.wait_recv()

    lens(blk, src_ref, shift_ref, taps_ref, ext, lensed_ref)

    pltpu.make_async_copy(others, others, send_a).wait()
    for copy in sent_b:
        copy.wait_send()
    for copy in sent_c:
        copy.wait_send()


def shards(spectra, source_tiles, tap_shift, kernels):
    spec = spectra.reshape(NBLK, 2, 2, 2, 2, 128).transpose(0, 1, 2, 4, 3, 5).reshape(NBLK, 16, 128)
    vmem = pl.BlockSpec(memory_space=pltpu.VMEM)
    smem = pl.BlockSpec(memory_space=pltpu.SMEM)
    shape = jax.ShapeDtypeStruct((8, 128, 128), F32)
    plain, lensed = pl.pallas_call(
        kernel,
        out_shape=(shape, shape),
        in_specs=[pl.BlockSpec(memory_space=pl.ANY), smem, smem] + [vmem] * 6,
        out_specs=(vmem, vmem),
        scratch_shapes=[
            pltpu.VMEM((16 * NBLK, 128), F32),
            pltpu.VMEM((NLON, 2, 2 * ROWS, 128), F32),
            pltpu.VMEM((3, 8, 2 * ROWS, 128), F32),
            pltpu.SemaphoreType.DMA((2,)),
            pltpu.SemaphoreType.DMA,
            pltpu.SemaphoreType.DMA,
            pltpu.SemaphoreType.DMA((NLON,)),
            pltpu.SemaphoreType.DMA((NLON,)),
            pltpu.SemaphoreType.DMA((2, NLON)),
            pltpu.SemaphoreType.DMA((2, NLON)),
        ],
        compiler_params=pltpu.CompilerParams(
            collective_id=0, has_side_effects=True, vmem_limit_bytes=40 * 1024 * 1024
        ),
    )(spec, source_tiles, tap_shift, kernels.reshape(16, 128), *map(jnp.asarray, tables()))

    def maps(x):
        return x.reshape(8, 64, 2, 128).transpose(0, 2, 1, 3).reshape(8, 2, 8192)

    return maps(plain), maps(lensed)


def solution(mesh):
    placed = (
        P(None, "lon", None, None, None, "blk"),
        P("blk", "lon", None),
        P("blk", "lon", None),
        P("blk", "lon", None, None),
    )
    return jax.shard_map(
        shards,
        mesh=mesh,
        in_specs=placed,
        out_specs=(P("blk", None, "lon"), P("blk", None, "lon")),
        check_vma=False,
    )
```

time: 165 us -> 56.6 us (0.34)
  local copies, waits for them, and re-layouts: 56.1 us -> 8.8 us
  Pallas kernels: 0 us -> 46.7 us
  blocking collectives: 30.9 us -> 0 us
  waiting for transfers between devices: 30.3 us -> 0 us
  matrix products: 18.3 us -> 0 us
  between operations: 14.4 us -> 0.65 us
  starting transfers between devices: 9.83 us -> 0 us
  other arithmetic: 3.96 us -> 0 us
    pallas_call x0 -> x1, Pallas kernels: none -> 46.7 us  [shards(): pl.pallas_call(kernel, out_shape=(shape, shape), in_specs=[pl.BlockSpec(m...]
    gather x65 -> x0, local copies, waits for them, and re-layouts: 34.4 us -> none
    all_to_all x1 -> x0, blocking collectives: 30.9 us -> none  [shards(): lax.all_to_all(spectra, 'blk', split_axis=0, concat_axis=5, tiled=True)]
    all_gather x1 -> x0, waiting for transfers between devices: 29.1 us -> none  [shards(): lax.all_gather(mine, 'lon', axis=0, tiled=True)]
    dot_general x7 -> x0, matrix products: 18.3 us -> none  [the longest x1 4.13 us: tile_values(): result = jnp.einsum('rcbu,qu->rcbq', triple, toeplitz, precision=HIGHEST)]
    ppermute x4 -> x0, starting transfers between devices: 9.79 us -> none  [the longest x2 6.23 us: padded(): lax.ppermute(lax.slice_in_dim(block, 0, width, axis=dim), axis, backward)]
    another operation x2 -> x0, local copies, waits for them, and re-layouts: 6.11 us -> none  [tile_values(): jnp.tile(placed, width)[:3 * width * width].reshape(width, 3 * width)]
    reshape x6 -> x0, local copies, waits for them, and re-layouts: 5.43 us -> none  [the longest x1 3.23 us: synthesize_cycles(): harmonic_spectrum.reshape(number_cycles, 2, 2, upper_order_digit, ORDER_R...]
  transfers between devices with their start and end apart: 5 -> 0, of which waited for: 2 -> 0; matrix products, arithmetic and copies ran while one was open for 26% -> 0% of each run, Pallas kernels for 0% -> 0%
where the time goes in v1:
time: 56.6 us; the launch traced here: 56.1 us
  Pallas kernels  46.7 us (83%)
  local copies, waits for them, and re-layouts  8.8 us (16%)
  between operations  0.65 us (1%)
    pallas_call x1, Pallas kernels, shards(): pl.pallas_call(kernel, out_shape=(shape, shape), in_specs=[pl.BlockSpec(m...  46.7 us
    unnamed x18, local copies, waits for them, and re-layouts  8.8 us

profile of v1, /device:TPU:1, one launch (start us, length us, event | category | flops | bytes accessed | tf_op | source)
XLA Modules:
  0.0 56.1 jit_solution(6285335360643341654)
XLA Ops:
  0.6 0.0 copy-start.6
  0.6 0.8 %copy.12.src_ref = s32[1,8,2]{2,1,0:T(8,128)S(1)} copy(s32[1,8,2]{1,2,0:T(2,128)} %param.10) | data formatting | bytes 128 | tf_op args[1]
  1.4 0.8 %copy.13.shift_ref = s32[1,8,2]{2,1,0:T(8,128)S(1)} copy(s32[1,8,2]{1,2,0:T(2,128)} %param.11) | data formatting | bytes 128 | tf_op args[2]
  2.2 0.0 copy-done.6
  2.2 0.0 copy-start
  2.2 1.0 %copy-done = f32[64,1,2,2,2,256]{5,4,3,2,1,0:T(2,128)S(1)} copy-done((f32[64,1,2,2,2,256]{5,4,3,2,1,0:T(2,128)S(1)}, f32[64,1,2,2,2,256]{5,4,3,2,1,0:T(2,128)}, u32[]{:S(2)}) %copy-start) | copy-done | bytes 524312
  3.2 0.0 copy-start.1
  3.2 1.0 %copy-done.1 = bf16[288,512]{1,0:T(8,128)(2,1)S(1)} copy-done((bf16[288,512]{1,0:T(8,128)(2,1)S(1)}, bf16[288,512]{1,0:T(8,128)(2,1)}, u32[]{:S(2)}) %copy-start.1) | copy-done | bytes 294936
  4.2 0.0 copy-start.2
  4.2 1.0 %copy-done.2 = bf16[288,512]{1,0:T(8,128)(2,1)S(1)} copy-done((bf16[288,512]{1,0:T(8,128)(2,1)S(1)}, bf16[288,512]{1,0:T(8,128)(2,1)}, u32[]{:S(2)}) %copy-start.2) | copy-done | bytes 294936
  5.1 0.0 copy-start.3
  5.1 0.9 %copy-done.3 = bf16[256,384]{1,0:T(8,128)(2,1)S(1)} copy-done((bf16[256,384]{1,0:T(8,128)(2,1)S(1)}, bf16[256,384]{1,0:T(8,128)(2,1)}, u32[]{:S(2)}) %copy-start.3) | copy-done | bytes 196632
  6.0 0.0 copy-start.4
  6.1 0.9 %copy-done.4 = f32[128,256]{1,0:T(8,128)S(1)} copy-done((f32[128,256]{1,0:T(8,128)S(1)}, f32[128,256]{1,0:T(8,128)}, u32[]{:S(2)}) %copy-start.4) | copy-done | bytes 131096
  7.0 0.0 copy-start.5
  7.0 0.9 %copy-done.5 = f32[128,256]{1,0:T(8,128)S(1)} copy-done((f32[128,256]{1,0:T(8,128)S(1)}, f32[128,256]{1,0:T(8,128)}, u32[]{:S(2)}) %copy-start.5) | copy-done | bytes 131096
  7.9 46.7 %shard_map.104 = (f32[8,128,128]{2,1,0:T(8,128)S(1)}, f32[8,128,128]{2,1,0:T(8,128)S(1)}) custom-call(f32[64,16,128]{2,1,0:T(8,128)S(1)} %bitcast.16, s32[1,8,2]{2,1,0:T(8,128)S(1)} %copy.12.src_ref, s32[1,8,2]{2,1,0:T(8,128)S(1)} %copy.13.shift_ref, f32[16,128]{1,0:T(8,128)S(1)} %bitcast.19, bf16[256,384]{1,0:T(8,128)(2,1)S(1)} %copy-done.3, ...), custom_call_target="tpu_custom_call" | custom-call | tf_op jit(solution)/shard_map/pallas_call | solution.py:226
  54.5 0.8 %copy.18 = f32[8,2,8192]{2,1,0:T(2,128)} copy(f32[8,2,8192]{2,1,0:T(2,128)S(1)} %bitcast.18) | data formatting | bytes 1048576
  55.3 0.8 %copy.19 = f32[8,2,8192]{2,1,0:T(2,128)} copy(f32[8,2,8192]{2,1,0:T(2,128)S(1)} %bitcast.17) | data formatting | bytes 1048576
Async XLA Ops:
  0.6 1.5 %copy-start.6 = (f32[1,8,2,128]{3,2,1,0:T(2,128)S(1)}, f32[1,8,2,128]{3,2,1,0:T(2,128)}, u32[]{:S(2)}) copy-start(f32[1,8,2,128]{3,2,1,0:T(2,128)} %param.12) | copy-start | bytes 24580
  2.2 1.0 %copy-start = (f32[64,1,2,2,2,256]{5,4,3,2,1,0:T(2,128)S(1)}, f32[64,1,2,2,2,256]{5,4,3,2,1,0:T(2,128)}, u32[]{:S(2)}) copy-start(f32[64,1,2,2,2,256]{5,4,3,2,1,0:T(2,128)} %param.9) | copy-start | bytes 1572868
  3.2 1.0 %copy-start.1 = (bf16[288,512]{1,0:T(8,128)(2,1)S(1)}, bf16[288,512]{1,0:T(8,128)(2,1)}, u32[]{:S(2)}) copy-start(bf16[288,512]{1,0:T(8,128)(2,1)} %constant.14.clone.low_ref) | copy-start | bytes 884740
  4.2 1.0 %copy-start.2 = (bf16[288,512]{1,0:T(8,128)(2,1)S(1)}, bf16[288,512]{1,0:T(8,128)(2,1)}, u32[]{:S(2)}) copy-start(bf16[288,512]{1,0:T(8,128)(2,1)} %constant.13.clone.high_ref) | copy-start | bytes 884740
  5.1 0.9 %copy-start.3 = (bf16[256,384]{1,0:T(8,128)(2,1)S(1)}, bf16[256,384]{1,0:T(8,128)(2,1)}, u32[]{:S(2)}) copy-start(bf16[256,384]{1,0:T(8,128)(2,1)} %constant.10.clone.first_ref) | copy-start | bytes 589828
  6.0 0.9 %copy-start.4 = (f32[128,256]{1,0:T(8,128)S(1)}, f32[128,256]{1,0:T(8,128)}, u32[]{:S(2)}) copy-start(f32[128,256]{1,0:T(8,128)} %constant.12.clone.sin_ref) | copy-start | bytes 393220
  7.0 0.9 %copy-start.5 = (f32[128,256]{1,0:T(8,128)S(1)}, f32[128,256]{1,0:T(8,128)}, u32[]{:S(2)}) copy-start(f32[128,256]{1,0:T(8,128)} %constant.11.clone.cos_ref) | copy-start | bytes 393220

commit v2 on v1

v2 whole, which is shorter than its diff:
```python
import math

import jax
import jax.numpy as jnp
import numpy as np
from jax import lax
from jax.experimental import pallas as pl
from jax.experimental.pallas import tpu as pltpu
from jax.sharding import PartitionSpec as P

NBLK = 64
NLON = 4
STAGE = 4
MESH = pl.DeviceIdType.MESH
F32 = jnp.float32
BF16 = jnp.bfloat16

ROWS = 72


def tables():
    def angle(rows, cols, period):
        return 2.0 * math.pi * ((rows[:, None] * cols[None, :]) % period) / period

    i = np.arange(128)
    b = np.arange(NBLK)
    n = np.arange(256)
    first = angle(i, b, 128)
    first = np.block([[np.cos(first), -np.sin(first)], [np.sin(first), np.cos(first)]])
    turn = angle(i, n, 32768)
    pixel_rows = np.concatenate([(64 * l + np.arange(ROWS) - 4) % 256 for l in range(NLON)])
    last = angle(pixel_rows, n, 256)
    last = np.concatenate([np.cos(last), -np.sin(last)], axis=1)
    return tuple(t.astype(np.float32) for t in (first, np.cos(turn), np.sin(turn), last))


def halves(x):
    high = x.astype(BF16)
    return high, (x - high.astype(F32)).astype(BF16)


def nt(a, b):
    return lax.dot_general(a, b, (((1,), (1,)), ((), ())), preferred_element_type=F32)


def synthesize(land, first_ref, cos_ref, sin_ref, high_ref, low_ref, made):
    for k in range(2):
        for q in range(2):
            kq = 2 * k + q
            parts = []
            for ri in range(2):
                rows = [land[pl.ds(4 * kq + 2 * h + ri, NBLK, stride=16), :] for h in range(2)]
                parts.append(jnp.concatenate(rows, axis=1))
            xh, xl = halves(jnp.concatenate(parts, axis=0))
            spread = jnp.concatenate([xh, xh, xl], axis=0)
            g = jnp.dot(first_ref[...], spread, preferred_element_type=F32)
            gre, gim = g[:128], g[128:]
            cos, sin = cos_ref[...], sin_ref[...]
            hh, hl = halves(
                jnp.concatenate([gre * cos - gim * sin, gre * sin + gim * cos], axis=1)
            )
            out = nt(high_ref[...], hh) + (nt(low_ref[...], hh) + nt(high_ref[...], hl))
            for l in range(NLON):
                made[l, k, pl.ds(q, ROWS, stride=2), :] = out[ROWS * l : ROWS * (l + 1)]


def base_of(shift):
    start = shift + 448
    base = jnp.clip(lax.shift_right_arithmetic(start, 7), 0, 6)
    return base, start - 128 * base


def place_taps(shift_ref, taps_ref, toep):
    q_index = lax.broadcasted_iota(jnp.int32, (128, 128), 0)
    u_index = lax.broadcasted_iota(jnp.int32, (128, 128), 1)
    lead = u_index - q_index

    def one(g, carry):
        for k in range(2):
            _, off = base_of(shift_ref[k, g])
            taps = jnp.broadcast_to(taps_ref[pl.ds(2 * g + k, 1), :], (8, 128))
            taps = pltpu.roll(taps, off & 127, 1)
            ring = pltpu.roll(
                jnp.broadcast_to(taps[:1], (128, 128)), 0, 1, stride=1, stride_axis=0
            )
            high = ring.astype(BF16).astype(F32)
            low = ring - high
            for i in range(3):
                at = lead + (128 * i - off)
                keep = (at >= 0) & (at < 128)
                toep[2 * g + k, :, 128 * i : 128 * i + 128] = jnp.where(keep, high, 0.0).astype(BF16)
                toep[2 * g + k, :, 128 * i + 384 : 128 * i + 512] = jnp.where(
                    keep, low, 0.0
                ).astype(BF16)
        return carry

    lax.fori_loop(0, 8, one, 0)


def kernel(
    spec_ref, shift_hbm, taps_hbm, first_hbm, cos_hbm, sin_hbm, last_hbm,
    ext, toep,
    land, made, shift_ref, taps_ref, first_ref, cos_ref, sin_ref, last_ref, first_cat, high_ref, low_ref,
    own_sem, send_a, recv_a, send_b, recv_b, send_c, recv_c,
):
    blk = lax.axis_index("blk")
    lon = lax.axis_index("lon")
    up = lax.rem(blk + 1, NBLK)
    down = lax.rem(blk + NBLK - 1, NBLK)

    barrier = pltpu.get_barrier_semaphore()

    def greet(o, carry):
        pl.semaphore_signal(
            barrier, inc=1, device_id=(lax.rem(blk + o, NBLK), lon), device_id_type=MESH
        )
        return carry

    lax.fori_loop(1, NBLK, greet, 0)
    for d in range(1, NLON):
        pl.semaphore_signal(
            barrier, inc=1, device_id=(blk, lax.rem(lon + d, NLON)), device_id_type=MESH
        )
    mine = pl.ds(pl.multiple_of(16 * blk, 16), 16)
    loads = [
        pltpu.make_async_copy(source, target, own_sem.at[j])
        for j, (source, target) in enumerate(
            (
                (spec_ref.at[blk], land.at[mine]),
                (shift_hbm, shift_ref),
                (taps_hbm, taps_ref),
                (first_hbm, first_ref),
                (cos_hbm, cos_ref),
                (sin_hbm, sin_ref),
                (last_hbm, last_ref),
            )
        )
    ]
    for load in loads:
        load.start()
    pl.semaphore_wait(barrier, NBLK - 1 + NLON - 1)

    def send(o, carry):
        to = lax.rem(blk + o, NBLK)
        pltpu.make_async_remote_copy(
            src_ref=spec_ref.at[to],
            dst_ref=land.at[mine],
            send_sem=send_a,
            recv_sem=recv_a,
            device_id=(to, lon),
            device_id_type=MESH,
        ).start()
        return carry

    if STAGE >= 1:
        lax.fori_loop(1, NBLK, send, 0)
    for load in loads:
        load.wait()
    place_taps(shift_ref, taps_ref, toep)
    fh, fl = halves(first_ref[...])
    first_cat[...] = jnp.concatenate([fh, fl, fh], axis=1)
    lh, ll = halves(last_ref[...])
    high_ref[...] = lh
    low_ref[...] = ll

    others = land.at[pl.ds(0, 16 * (NBLK - 1))]
    if STAGE >= 1:
        pltpu.make_async_copy(others, others, recv_a).wait()

    if STAGE >= 2:
        synthesize(land, first_cat, cos_ref, sin_ref, high_ref, low_ref, made)

    def across(d):
        to = lax.rem(lon + d, NLON)
        return pltpu.make_async_remote_copy(
            src_ref=made.at[to],
            dst_ref=ext.at[1, pl.ds(2 * lon, 2)],
            send_sem=send_b.at[d],
            recv_sem=recv_b.at[d],
            device_id=(blk, to),
            device_id_type=MESH,
        )

    def beside(d, source, l, to, slot, side):
        return pltpu.make_async_remote_copy(
            src_ref=source,
            dst_ref=ext.at[slot, pl.ds(2 * l, 2)],
            send_sem=send_c.at[side, d],
            recv_sem=recv_c.at[side, d],
            device_id=(to, lon),
            device_id_type=MESH,
        )

    sent_b = [across(d) for d in (1, 3, 2)] if STAGE >= 3 else []
    for copy in sent_b:
        copy.start()
    sent_c = []
    for d in (0, 1, 3, 2):
        l = lax.rem(lon + NLON - d, NLON)
        if d == 0:
            source = made.at[lon]
            keep = pltpu.make_async_copy(source, ext.at[1, pl.ds(2 * lon, 2)], own_sem.at[7])
            keep.start()
        else:
            if STAGE >= 3:
                across(d).wait_recv()
            source = ext.at[1, pl.ds(2 * l, 2)]
        if STAGE < 4:
            continue
        for to, slot, side in ((up, 0, 0), (down, 2, 1)):
            copy = beside(d, source, l, to, slot, side)
            copy.start()
            sent_c.append(copy)
    keep.wait()
    for copy in sent_c:
        copy.wait_recv()
    if STAGE >= 1:
        pltpu.make_async_copy(others, others, send_a).wait()
    for copy in sent_b:
        copy.wait_send()
    for copy in sent_c:
        copy.wait_send()


def lens_kernel(
    src_hbm, shift_hbm, ext, toep, plain_ref, lensed_ref, src_ref, shift_ref, out, sems, out_sem
):
    blk = lax.axis_index("blk")
    loads = [
        pltpu.make_async_copy(src_hbm, src_ref, sems.at[0]),
        pltpu.make_async_copy(shift_hbm, shift_ref, sems.at[1]),
    ]
    for load in loads:
        load.start()
    keep = pltpu.make_async_copy(ext.at[1, :, pl.ds(8, 128), :], plain_ref, sems.at[2])
    keep.start()
    for load in loads:
        load.wait()
    copies = []
    for g in range(8):
        total = None
        for k in range(2):
            which = jnp.clip(src_ref[k, g] - blk + 1, 0, 2)
            base, _ = base_of(shift_ref[k, g])
            wins = []
            for i in range(3):
                row = 2 * (8 * g + base + i)
                wins.append(
                    jnp.concatenate(
                        [ext[which, u, pl.ds(row, 16), :] for u in range(8)], axis=0
                    )
                )
            wh, wl = halves(jnp.concatenate(wins, axis=1))
            th, tl = toep[2 * g + k, :, :384], toep[2 * g + k, :, 384:]
            part = nt(wh, th) + (nt(wl, th) + nt(wh, tl))
            total = part if total is None else total + part
        rows = pl.ds(16 * g, 16)
        out[:, rows, :] = total.reshape(8, 16, 128)
        copy = pltpu.make_async_copy(out.at[:, rows, :], lensed_ref.at[:, rows, :], out_sem.at[g])
        copy.start()
        copies.append(copy)
    keep.wait()
    for copy in copies:
        copy.wait()


def shards(spectra, source_tiles, tap_shift, kernels):
    spec = spectra.reshape(NBLK, 2, 2, 2, 2, 128).transpose(0, 1, 2, 4, 3, 5).reshape(NBLK, 16, 128)
    sources = source_tiles.transpose(0, 2, 1).reshape(2, 8)
    shifts = tap_shift.transpose(0, 2, 1).reshape(2, 8)
    vmem = pl.BlockSpec(memory_space=pltpu.VMEM)
    smem = pl.BlockSpec(memory_space=pltpu.SMEM)
    hbm = pl.BlockSpec(memory_space=pltpu.HBM)
    dma = pltpu.SemaphoreType.DMA
    ext, toep = pl.pallas_call(
        kernel,
        out_shape=(
            jax.ShapeDtypeStruct((3, 8, 2 * ROWS, 128), F32),
            jax.ShapeDtypeStruct((16, 128, 768), BF16),
        ),
        in_specs=[hbm] * 7,
        out_specs=(vmem, vmem),
        scratch_shapes=[
            pltpu.VMEM((16 * NBLK, 128), F32),
            pltpu.VMEM((NLON, 2, 2 * ROWS, 128), F32),
            pltpu.SMEM((2, 8), jnp.int32),
            pltpu.VMEM((16, 128), F32),
            pltpu.VMEM((256, 128), F32),
            pltpu.VMEM((128, 256), F32),
            pltpu.VMEM((128, 256), F32),
            pltpu.VMEM((NLON * ROWS, 512), F32),
            pltpu.VMEM((256, 384), BF16),
            pltpu.VMEM((NLON * ROWS, 512), BF16),
            pltpu.VMEM((NLON * ROWS, 512), BF16),
            dma((8,)),
            dma,
            dma,
            dma((NLON,)),
            dma((NLON,)),
            dma((2, NLON)),
            dma((2, NLON)),
        ],
        compiler_params=pltpu.CompilerParams(
            collective_id=0, has_side_effects=True, vmem_limit_bytes=32 * 1024 * 1024
        ),
    )(*(pltpu.with_memory_space_constraint(x, pltpu.HBM) for x in (spec, shifts, kernels.reshape(16, 128), *map(jnp.asarray, tables()))))
    shape = jax.ShapeDtypeStruct((8, 128, 128), F32)
    plain, lensed = pl.pallas_call(
        lens_kernel,
        out_shape=(shape, shape),
        in_specs=[hbm, hbm, vmem, vmem],
        out_specs=(hbm, hbm),
        scratch_shapes=[
            pltpu.SMEM((2, 8), jnp.int32),
            pltpu.SMEM((2, 8), jnp.int32),
            pltpu.VMEM((8, 128, 128), F32),
            dma((3,)),
            dma((8,)),
        ],
        compiler_params=pltpu.CompilerParams(vmem_limit_bytes=32 * 1024 * 1024),
    )(*(pltpu.with_memory_space_constraint(x, pltpu.HBM) for x in (sources, shifts)), ext, toep)

    def maps(x):
        return x.reshape(8, 64, 2, 128).transpose(0, 2, 1, 3).reshape(8, 2, 8192)

    return maps(plain), maps(lensed)


def solution(mesh):
    placed = (
        P(None, "lon", None, None, None, "blk"),
        P("blk", "lon", None),
        P("blk", "lon", None),
        P("blk", "lon", None, None),
    )
    return jax.shard_map(
        shards,
        mesh=mesh,
        in_specs=placed,
        out_specs=(P("blk", None, "lon"), P("blk", None, "lon")),
        check_vma=False,
    )
```

time: 56.6 us -> 46 us (0.81)
  local copies, waits for them, and re-layouts: 8.8 us -> 0 us
  Pallas kernels: 46.7 us -> 45.2 us
    unnamed x18 -> x0, local copies, waits for them, and re-layouts: 8.8 us -> none
    pallas_call x1 -> x2, Pallas kernels: 46.7 us -> 45.2 us  [the longest x1 41.6 us: shards(): pl.pallas_call(kernel, out_shape=(jax.ShapeDtypeStruct((3, 8, 2 * ROWS, 1...]
where the time goes in v2:
time: 46 us; the launch traced here: 45.8 us
  Pallas kernels  45.2 us (98%)
  between operations  0.64 us (1%)
    pallas_call x1, Pallas kernels, shards(): pl.pallas_call(kernel, out_shape=(jax.ShapeDtypeStruct((3, 8, 2 * ROWS, 1...  41.6 us
    pallas_call x1, Pallas kernels, shards(): pl.pallas_call(lens_kernel, out_shape=(shape, shape), in_specs=[hbm, hbm,...  3.56 us

profile of v2, /device:TPU:1, one launch (start us, length us, event | category | flops | bytes accessed | tf_op | source)
XLA Modules:
  0.0 45.8 jit_solution(4766143723668671160)
XLA Ops:
  0.6 41.6 %shard_map.95 = (f32[3,8,144,128]{3,2,1,0:T(8,128)S(1)}, bf16[16,128,768]{2,1,0:T(8,128)(2,1)S(1)}) custom-call(f32[64,16,128]{2,1,0:T(8,128)} %bitcast.22, s32[2,8]{1,0:T(2,128)} %bitcast.24, f32[16,128]{1,0:T(8,128)} %bitcast.23, f32[256,128]{1,0:T(8,128)} %constant.8.clone.first_hbm, f32[128,256]{1,0:T(8,128)} %constant.9.clone.cos_hbm, ...), custom_call_target="tpu_custom_call" | custom-call | tf_op jit(solution)/shard_map/pallas_call | solution.py:275
  42.2 3.6 %shard_map.96 = (f32[8,128,128]{2,1,0:T(8,128)}, f32[8,128,128]{2,1,0:T(8,128)}) custom-call(s32[2,8]{1,0:T(2,128)} %bitcast.26, s32[2,8]{1,0:T(2,128)} %bitcast.25, f32[3,8,144,128]{3,2,1,0:T(8,128)S(1)} %get-tuple-element.6.ext, bf16[16,128,768]{2,1,0:T(8,128)(2,1)S(1)} %get-tuple-element.7.toep), custom_call_target="tpu_custom_call" | custom-call | tf_op jit(solution)/shard_map/pallas_call | solution.py:308

commit v3 on v2

v3 whole, which is shorter than its diff:
```python
import functools
import math

import jax
import jax.numpy as jnp
import numpy as np
from jax import lax
from jax.experimental import pallas as pl
from jax.experimental.pallas import tpu as pltpu
from jax.sharding import PartitionSpec as P

NBLK = 64
NLON = 4
MESH = pl.DeviceIdType.MESH
F32 = jnp.float32
BF16 = jnp.bfloat16

ROWS = 72


def tables():
    def angle(rows, cols, period):
        return 2.0 * math.pi * ((rows[:, None] * cols[None, :]) % period) / period

    i = np.arange(128)
    b = np.arange(NBLK)
    n = np.arange(256)
    first = angle(i, b, 128)
    first = np.block([[np.cos(first), -np.sin(first)], [np.sin(first), np.cos(first)]])
    turn = angle(i, n, 32768)
    pixel_rows = np.concatenate([(64 * l + np.arange(ROWS) - 4) % 256 for l in range(NLON)])
    last = angle(pixel_rows, n, 256)
    last = np.concatenate([np.cos(last), -np.sin(last)], axis=1)
    return tuple(t.astype(np.float32) for t in (first, np.cos(turn), np.sin(turn), last))


def halves(x):
    high = x.astype(BF16)
    return high, (x - high.astype(F32)).astype(BF16)


def nt(a, b):
    return lax.dot_general(a, b, (((1,), (1,)), ((), ())), preferred_element_type=F32)


def synthesize(k, land, first_ref, cos_ref, sin_ref, high_ref, low_ref, made):
    for q in range(2):
        parts = []
        for ri in range(2):
            rows = [land[k, pl.ds(4 * q + 2 * h + ri, NBLK, stride=8), :] for h in range(2)]
            parts.append(jnp.concatenate(rows, axis=1))
        xh, xl = halves(jnp.concatenate(parts, axis=0))
        spread = jnp.concatenate([xh, xh, xl], axis=0)
        g = jnp.dot(first_ref[...], spread, preferred_element_type=F32)
        gre, gim = g[:128], g[128:]
        cos, sin = cos_ref[...], sin_ref[...]
        hh, hl = halves(jnp.concatenate([gre * cos - gim * sin, gre * sin + gim * cos], axis=1))
        out = nt(high_ref[...], hh) + (nt(low_ref[...], hh) + nt(high_ref[...], hl))
        for l in range(NLON):
            made[k, l, pl.ds(q, ROWS, stride=2), :] = out[ROWS * l : ROWS * (l + 1)]


def base_of(shift):
    start = shift + 448
    base = jnp.clip(lax.shift_right_arithmetic(start, 7), 0, 6)
    return base, start - 128 * base


def place_taps(shift_ref, taps_ref, toep):
    q_index = lax.broadcasted_iota(jnp.int32, (128, 128), 0)
    u_index = lax.broadcasted_iota(jnp.int32, (128, 128), 1)
    lead = u_index - q_index

    def one(g, carry):
        for k in range(2):
            _, off = base_of(shift_ref[k, g])
            taps = jnp.broadcast_to(taps_ref[pl.ds(2 * g + k, 1), :], (8, 128))
            taps = pltpu.roll(taps, off & 127, 1)
            ring = pltpu.roll(
                jnp.broadcast_to(taps[:1], (128, 128)), 0, 1, stride=1, stride_axis=0
            )
            high = ring.astype(BF16).astype(F32)
            low = ring - high
            for i in range(3):
                at = lead + (128 * i - off)
                keep = (at >= 0) & (at < 128)
                toep[2 * g + k, :, 128 * i : 128 * i + 128] = jnp.where(keep, high, 0.0).astype(BF16)
                toep[2 * g + k, :, 128 * i + 384 : 128 * i + 512] = jnp.where(
                    keep, low, 0.0
                ).astype(BF16)
        return carry

    lax.fori_loop(0, 8, one, 0)


def lens(k, tiles, blk, src_ref, shift_ref, ext, toep, lensed_ref):
    for g in tiles:
        total = None
        for j in range(2):
            which = jnp.clip(src_ref[j, g] - blk + 1, 0, 2)
            base, _ = base_of(shift_ref[j, g])
            wins = []
            for i in range(3):
                row = 2 * (8 * g + base + i)
                wins.append(
                    jnp.concatenate(
                        [ext[k][which, l, pl.ds(row, 16), :] for l in range(NLON)], axis=0
                    )
                )
            wh, wl = halves(jnp.concatenate(wins, axis=1))
            th, tl = toep[2 * g + j, :, :384], toep[2 * g + j, :, 384:]
            part = nt(wh, th) + (nt(wl, th) + nt(wh, tl))
            total = part if total is None else total + part
        for l in range(NLON):
            lensed_ref[l, k, 16 * g : 16 * g + 16, :] = total[16 * l : 16 * l + 16]


def kernel(
    spec_ref, src_hbm, shift_hbm, taps_hbm, first_hbm, cos_hbm, sin_hbm, last_hbm,
    ext_0, ext_1, lensed_ref,
    land, made, toep, src_ref, shift_ref, taps_ref, first_ref, cos_ref, sin_ref, last_ref,
    first_cat, high_ref, low_ref,
    own_sem, send_a, recv_a, send_b, recv_b, send_c, recv_c,
):
    ext = (ext_0, ext_1)
    blk = lax.axis_index("blk")
    lon = lax.axis_index("lon")
    up = lax.rem(blk + 1, NBLK)
    down = lax.rem(blk + NBLK - 1, NBLK)

    barrier = pltpu.get_barrier_semaphore()

    def greet(o, carry):
        pl.semaphore_signal(
            barrier, inc=1, device_id=(lax.rem(blk + o, NBLK), lon), device_id_type=MESH
        )
        return carry

    lax.fori_loop(1, NBLK, greet, 0)
    for d in range(1, NLON):
        pl.semaphore_signal(
            barrier, inc=1, device_id=(blk, lax.rem(lon + d, NLON)), device_id_type=MESH
        )
    mine = pl.ds(pl.multiple_of(8 * blk, 8), 8)
    loads = [
        pltpu.make_async_copy(source, target, own_sem.at[j])
        for j, (source, target) in enumerate(
            (
                (spec_ref.at[blk, 0], land.at[0, mine]),
                (spec_ref.at[blk, 1], land.at[1, mine]),
                (src_hbm, src_ref),
                (shift_hbm, shift_ref),
                (taps_hbm, taps_ref),
                (first_hbm, first_ref),
                (cos_hbm, cos_ref),
                (sin_hbm, sin_ref),
                (last_hbm, last_ref),
            )
        )
    ]
    for load in loads:
        load.start()
    pl.semaphore_wait(barrier, NBLK - 1 + NLON - 1)

    for k in range(2):

        def send(o, carry, k=k):
            to = lax.rem(blk + o, NBLK)
            pltpu.make_async_remote_copy(
                src_ref=spec_ref.at[to, k],
                dst_ref=land.at[k, mine],
                send_sem=send_a.at[k],
                recv_sem=recv_a.at[k],
                device_id=(to, lon),
                device_id_type=MESH,
            ).start()
            return carry

        lax.fori_loop(1, NBLK, send, 0)

    for load in loads:
        load.wait()
    place_taps(shift_ref, taps_ref, toep)
    fh, fl = halves(first_ref[...])
    first_cat[...] = jnp.concatenate([fh, fl, fh], axis=1)
    lh, ll = halves(last_ref[...])
    high_ref[...] = lh
    low_ref[...] = ll

    others = [land.at[k, pl.ds(0, 8 * (NBLK - 1))] for k in range(2)]

    def across(k, d):
        to = lax.rem(lon + d, NLON)
        return pltpu.make_async_remote_copy(
            src_ref=made.at[k, to],
            dst_ref=ext[k].at[1, lon],
            send_sem=send_b.at[k, d],
            recv_sem=recv_b.at[k, d],
            device_id=(blk, to),
            device_id_type=MESH,
        )

    def beside(k, d, source, to, slot, side):
        l = lax.rem(lon + NLON - d, NLON)
        return pltpu.make_async_remote_copy(
            src_ref=source,
            dst_ref=ext[k].at[slot, l],
            send_sem=send_c.at[k, side, d],
            recv_sem=recv_c.at[k, side, d],
            device_id=(to, lon),
            device_id_type=MESH,
        )

    sent = []
    landed = [[], []]
    kept = []

    def forward(k, d):
        if d == 0:
            source = made.at[k, lon]
            keep = pltpu.make_async_copy(source, ext[k].at[1, lon], own_sem.at[9 + k])
            keep.start()
            kept.append(keep)
        else:
            across(k, d).wait_recv()
            source = ext[k].at[1, lax.rem(lon + NLON - d, NLON)]
        for to, slot, side in ((up, 0, 0), (down, 2, 1)):
            copy = beside(k, d, source, to, slot, side)
            copy.start()
            sent.append(copy)
            landed[k].append(copy)

    def turn(k):
        pltpu.make_async_copy(others[k], others[k], recv_a.at[k]).wait()
        synthesize(k, land, first_cat, cos_ref, sin_ref, high_ref, low_ref, made)
        for d in (2, 1, 3):
            copy = across(k, d)
            copy.start()
            sent.append(copy)
        forward(k, 0)

    turn(0)
    for d in (1, 3, 2):
        forward(0, d)
    turn(1)
    kept[0].wait()
    for copy in landed[0]:
        copy.wait_recv()
    first_part = functools.partial(
        lens, 0, blk=blk, src_ref=src_ref, shift_ref=shift_ref, ext=ext, toep=toep,
        lensed_ref=lensed_ref,
    )
    first_part(tiles=range(0, 3))
    forward(1, 1)
    first_part(tiles=range(3, 6))
    forward(1, 3)
    first_part(tiles=range(6, 8))
    forward(1, 2)
    kept[1].wait()
    for copy in landed[1]:
        copy.wait_recv()
    lens(1, range(8), blk, src_ref, shift_ref, ext, toep, lensed_ref)
    for k in range(2):
        pltpu.make_async_copy(others[k], others[k], send_a.at[k]).wait()
    for copy in sent:
        copy.wait_send()


def finish(ext_0, ext_1, lensed_vmem, plain_ref, lensed_ref, sems):
    copies = [
        pltpu.make_async_copy(ext_0.at[1, :, pl.ds(8, 128), :], plain_ref.at[:, 0], sems.at[0]),
        pltpu.make_async_copy(ext_1.at[1, :, pl.ds(8, 128), :], plain_ref.at[:, 1], sems.at[1]),
        pltpu.make_async_copy(lensed_vmem, lensed_ref, sems.at[2]),
    ]
    for copy in copies:
        copy.start()
    for copy in copies:
        copy.wait()


def shards(spectra, source_tiles, tap_shift, kernels):
    spec = spectra.reshape(NBLK, 2, 2, 2, 2, 128).transpose(0, 1, 2, 4, 3, 5).reshape(NBLK, 2, 8, 128)
    operands = (
        spec,
        source_tiles.transpose(0, 2, 1).reshape(2, 8),
        tap_shift.transpose(0, 2, 1).reshape(2, 8),
        kernels.reshape(16, 128),
        *map(jnp.asarray, tables()),
    )
    vmem = pl.BlockSpec(memory_space=pltpu.VMEM)
    hbm = pl.BlockSpec(memory_space=pltpu.HBM)
    dma = pltpu.SemaphoreType.DMA
    shape = jax.ShapeDtypeStruct((NLON, 2, 128, 128), F32)
    ext_0, ext_1, lensed = pl.pallas_call(
        kernel,
        out_shape=(*[jax.ShapeDtypeStruct((3, NLON, 2 * ROWS, 128), F32)] * 2, shape),
        in_specs=[hbm] * 8,
        out_specs=(vmem,) * 3,
        scratch_shapes=[
            pltpu.VMEM((2, 8 * NBLK, 128), F32),
            pltpu.VMEM((2, NLON, 2 * ROWS, 128), F32),
            pltpu.VMEM((16, 128, 768), BF16),
            pltpu.SMEM((2, 8), jnp.int32),
            pltpu.SMEM((2, 8), jnp.int32),
            pltpu.VMEM((16, 128), F32),
            pltpu.VMEM((256, 128), F32),
            pltpu.VMEM((128, 256), F32),
            pltpu.VMEM((128, 256), F32),
            pltpu.VMEM((NLON * ROWS, 512), F32),
            pltpu.VMEM((256, 384), BF16),
            pltpu.VMEM((NLON * ROWS, 512), BF16),
            pltpu.VMEM((NLON * ROWS, 512), BF16),
            dma((11,)),
            dma((2,)),
            dma((2,)),
            dma((2, NLON)),
            dma((2, NLON)),
            dma((2, 2, NLON)),
            dma((2, 2, NLON)),
        ],
        compiler_params=pltpu.CompilerParams(
            collective_id=0, has_side_effects=True, vmem_limit_bytes=32 * 1024 * 1024
        ),
    )(*(pltpu.with_memory_space_constraint(x, pltpu.HBM) for x in operands))
    plain, lensed = pl.pallas_call(
        finish,
        out_shape=(shape, shape),
        in_specs=[vmem] * 3,
        out_specs=(hbm, hbm),
        scratch_shapes=[dma((3,))],
        compiler_params=pltpu.CompilerParams(vmem_limit_bytes=16 * 1024 * 1024),
    )(ext_0, ext_1, lensed)

    def maps(x):
        return x.reshape(8, 64, 2, 128).transpose(0, 2, 1, 3).reshape(8, 2, 8192)

    return maps(plain), maps(lensed)


def solution(mesh):
    placed = (
        P(None, "lon", None, None, None, "blk"),
        P("blk", "lon", None),
        P("blk", "lon", None),
        P("blk", "lon", None, None),
    )
    return jax.shard_map(
        shards,
        mesh=mesh,
        in_specs=placed,
        out_specs=(P("blk", None, "lon"), P("blk", None, "lon")),
        check_vma=False,
    )
```

time: 46 us -> 45.2 us (0.983)
  Pallas kernels: 45.2 us -> 44 us
    pallas_call x2, Pallas kernels: 45.2 us -> 44 us  [the longest x1 43 us: shards(): pl.pallas_call(kernel, out_shape=(*[jax.ShapeDtypeStruct((3, NLON, 2 * RO...]
where the time goes in v3:
time: 45.2 us; the launch traced here: 44.6 us
  Pallas kernels  44 us (97%)
  between operations  0.64 us (1%)
    pallas_call x1, Pallas kernels, shards(): pl.pallas_call(kernel, out_shape=(*[jax.ShapeDtypeStruct((3, NLON, 2 * RO...  43 us
    pallas_call x1, Pallas kernels, shards(): pl.pallas_call(finish, out_shape=(shape, shape), in_specs=[vmem] * 3, out...  1 us

profile of v3, /device:TPU:1, one launch (start us, length us, event | category | flops | bytes accessed | tf_op | source)
XLA Modules:
  0.0 44.6 jit_solution(11174589466038280658)
XLA Ops:
  0.6 43.0 %shard_map.95 = (f32[3,4,144,128]{3,2,1,0:T(8,128)S(1)}, f32[3,4,144,128]{3,2,1,0:T(8,128)S(1)}, f32[4,2,128,128]{3,2,1,0:T(8,128)S(1)}) custom-call(f32[64,2,8,128]{3,2,1,0:T(8,128)} %bitcast.22, s32[2,8]{1,0:T(2,128)} %bitcast.24, s32[2,8]{1,0:T(2,128)} %bitcast.25, f32[16,128]{1,0:T(8,128)} %bitcast.23, f32[256,128]{1,0:T(8,128)} %constant.8.clone.first_hbm, ...), custom_call_target="tpu_custom_call" | custom-call | tf_op jit(solution)/shard_map/pallas_call | solution.py:294
  43.6 1.0 %shard_map.96 = (f32[4,2,128,128]{3,2,1,0:T(8,128)}, f32[4,2,128,128]{3,2,1,0:T(8,128)}) custom-call(f32[3,4,144,128]{3,2,1,0:T(8,128)S(1)} %get-tuple-element.7.ext_0, f32[3,4,144,128]{3,2,1,0:T(8,128)S(1)} %get-tuple-element.8.ext_1, f32[4,2,128,128]{3,2,1,0:T(8,128)S(1)} %get-tuple-element.9.lensed_vmem), custom_call_target="tpu_custom_call" | custom-call | tf_op jit(solution)/shard_map/pallas_call | solution.py:325

commit v4 on v3

v4 whole, which is shorter than its diff:
```python
import math

import jax
import jax.numpy as jnp
import numpy as np
from jax import lax
from jax.experimental import pallas as pl
from jax.experimental.pallas import tpu as pltpu
from jax.sharding import PartitionSpec as P

NBLK = 64
NLON = 4
PARTS = 4
MESH = pl.DeviceIdType.MESH
F32 = jnp.float32
BF16 = jnp.bfloat16

ROWS = 72


def tables():
    def angle(rows, cols, period):
        return 2.0 * math.pi * ((rows[:, None] * cols[None, :]) % period) / period

    i = np.arange(128)
    b = np.arange(NBLK)
    n = np.arange(256)
    turn = angle(i, b, 128)
    first = np.zeros((2, 2, 128, NBLK, 2, 2))
    for h in range(2):
        first[h, 0, :, :, h, 0] = np.cos(turn)
        first[h, 0, :, :, h, 1] = -np.sin(turn)
        first[h, 1, :, :, h, 0] = np.sin(turn)
        first[h, 1, :, :, h, 1] = np.cos(turn)
    first = first.reshape(512, 256)
    turn = angle(i, n, 32768)
    pixel_rows = np.concatenate([(64 * l + np.arange(ROWS) - 4) % 256 for l in range(NLON)])
    last = angle(pixel_rows, n, 256)
    last = np.concatenate([np.cos(last), -np.sin(last)], axis=1)
    return tuple(t.astype(np.float32) for t in (first, np.cos(turn), np.sin(turn), last))


def halves(x):
    high = x.astype(BF16)
    return high, (x - high.astype(F32)).astype(BF16)


def dot(a, b):
    return jnp.dot(a, b, preferred_element_type=F32)


def nt(a, b):
    return lax.dot_general(a, b, (((1,), (1,)), ((), ())), preferred_element_type=F32)


def synthesize(p, land, first_ref, cos_ref, sin_ref, high_ref, low_ref, made):
    xh, xl = halves(land[p].reshape(4 * NBLK, 128))
    g = dot(first_ref[...], jnp.concatenate([xh, xh, xl], axis=0))
    real, imag = [], []
    for h in range(2):
        gre, gim = g[256 * h : 256 * h + 128], g[256 * h + 128 : 256 * h + 256]
        cos, sin = cos_ref[:, 128 * h : 128 * h + 128], sin_ref[:, 128 * h : 128 * h + 128]
        real.append(gre * cos - gim * sin)
        imag.append(gre * sin + gim * cos)
    hh, hl = halves(jnp.concatenate(real + imag, axis=1))
    out = nt(high_ref[...], hh) + (nt(low_ref[...], hh) + nt(high_ref[...], hl))
    made[p] = out.reshape(NLON, ROWS, 128)


def base_of(shift):
    start = shift + 448
    base = jnp.clip(lax.shift_right_arithmetic(start, 7), 0, 6)
    return base, start - 128 * base


def place_taps(shift_ref, taps_ref, toep):
    lane = lax.broadcasted_iota(jnp.int32, (128, 128), 1)
    row = lax.broadcasted_iota(jnp.int32, (128, 128), 0)
    lead = row - lane
    flip = jnp.where(row + lane == 127, 1.0, 0.0).astype(BF16)
    high, low = halves(taps_ref[:16])
    taps_ref[...] = jnp.concatenate([dot(high, flip), dot(low, flip)], axis=0)

    def one(g, carry):
        for j in range(2):
            _, off = base_of(shift_ref[j, g])
            for half in range(2):
                taps = taps_ref[pl.ds(16 * half + 2 * g + j, 1), :]
                taps = pltpu.roll(jnp.broadcast_to(taps, (8, 128)), (129 - off) & 127, 1)
                ring = pltpu.roll(
                    jnp.broadcast_to(taps[:1], (128, 128)), 0, 1, stride=1, stride_axis=0
                )
                for i in range(3):
                    at = lead + (128 * i - off)
                    rows = slice(384 * j + 128 * i, 384 * j + 128 * i + 128)
                    toep[g, rows, 128 * half : 128 * half + 128] = jnp.where(
                        (at >= 0) & (at < 128), ring, 0.0
                    ).astype(BF16)
        return carry

    lax.fori_loop(0, 8, one, 0)


def lens(p, blk, src_ref, shift_ref, ext, toep, lensed_ref):
    for g in range(8):
        wins = []
        for j in range(2):
            which = jnp.clip(src_ref[j, g] - blk + 1, 0, 2)
            base, _ = base_of(shift_ref[j, g])
            for i in range(3):
                rows = pl.ds(8 * g + base + i, 8)
                wins.append(
                    jnp.concatenate([ext[which, l, rows, :] for l in range(NLON)], axis=0)
                )
        high, low = halves(jnp.concatenate(wins, axis=1))
        r = dot(jnp.concatenate([high, low], axis=0), toep[g])
        r = r[:, :128] + r[:, 128:]
        r = r[: 8 * NLON] + r[8 * NLON :]
        for l in range(NLON):
            lensed_ref[l, p // 2, pl.ds(16 * g + p % 2, 8, stride=2), :] = r[8 * l : 8 * l + 8]


def kernel(
    spec_ref, src_hbm, shift_hbm, taps_hbm, first_hbm, cos_hbm, sin_hbm, last_hbm,
    plain_ref, lensed_ref,
    ext_0, ext_1, ext_2, ext_3, land, made, toep, src_ref, shift_ref, taps_ref,
    first_ref, cos_ref, sin_ref, last_ref, first_cat, high_ref, low_ref,
    own_sem, send_a, recv_a, send_b, recv_b, send_c, recv_c,
):
    ext = (ext_0, ext_1, ext_2, ext_3)
    blk = lax.axis_index("blk")
    lon = lax.axis_index("lon")
    up = lax.rem(blk + 1, NBLK)
    down = lax.rem(blk + NBLK - 1, NBLK)

    barrier = pltpu.get_barrier_semaphore()

    def greet(o, carry):
        pl.semaphore_signal(
            barrier, inc=1, device_id=(lax.rem(blk + o, NBLK), lon), device_id_type=MESH
        )
        return carry

    lax.fori_loop(1, NBLK, greet, 0)
    for d in range(1, NLON):
        pl.semaphore_signal(
            barrier, inc=1, device_id=(blk, lax.rem(lon + d, NLON)), device_id_type=MESH
        )
    loads = [
        pltpu.make_async_copy(source, target, own_sem.at[j])
        for j, (source, target) in enumerate(
            [(spec_ref.at[blk, p], land.at[p, blk]) for p in range(PARTS)]
            + [
                (src_hbm, src_ref),
                (shift_hbm, shift_ref),
                (taps_hbm, taps_ref.at[pl.ds(0, 16)]),
                (first_hbm, first_ref),
                (cos_hbm, cos_ref),
                (sin_hbm, sin_ref),
                (last_hbm, last_ref),
            ]
        )
    ]
    for load in loads:
        load.start()
    pl.semaphore_wait(barrier, NBLK - 1 + NLON - 1)

    for p in range(PARTS):

        def send(o, carry, p=p):
            to = lax.rem(blk + o, NBLK)
            pltpu.make_async_remote_copy(
                src_ref=spec_ref.at[to, p],
                dst_ref=land.at[p, blk],
                send_sem=send_a.at[p],
                recv_sem=recv_a.at[p],
                device_id=(to, lon),
                device_id_type=MESH,
            ).start()
            return carry

        lax.fori_loop(1, NBLK, send, 0)

    for load in loads:
        load.wait()
    fh, fl = halves(first_ref[...])
    first_cat[...] = jnp.concatenate([fh, fl, fh], axis=1)
    lh, ll = halves(last_ref[...])
    high_ref[...] = lh
    low_ref[...] = ll
    place_taps(shift_ref, taps_ref, toep)

    others = [land.at[p, pl.ds(0, NBLK - 1)] for p in range(PARTS)]

    def across(p, d):
        to = lax.rem(lon + d, NLON)
        return pltpu.make_async_remote_copy(
            src_ref=made.at[p, to],
            dst_ref=ext[p].at[1, lon],
            send_sem=send_b.at[p, d],
            recv_sem=recv_b.at[p, d],
            device_id=(blk, to),
            device_id_type=MESH,
        )

    def beside(p, d, source, to, slot, side):
        l = lax.rem(lon + NLON - d, NLON)
        return pltpu.make_async_remote_copy(
            src_ref=source,
            dst_ref=ext[p].at[slot, l],
            send_sem=send_c.at[p, side, d],
            recv_sem=recv_c.at[p, side, d],
            device_id=(to, lon),
            device_id_type=MESH,
        )

    sent = []
    landed = [[] for _ in range(PARTS)]

    def forward(p, d):
        if d == 0:
            source = made.at[p, lon]
            keep = pltpu.make_async_copy(source, ext[p].at[1, lon], own_sem.at[11 + p])
            keep.start()
            landed[p].append(keep.wait)
        else:
            across(p, d).wait_recv()
            source = ext[p].at[1, lax.rem(lon + NLON - d, NLON)]
        for to, slot, side in ((up, 0, 0), (down, 2, 1)):
            copy = beside(p, d, source, to, slot, side)
            copy.start()
            sent.append(copy)
            landed[p].append(copy.wait_recv)

    def turn(p):
        pltpu.make_async_copy(others[p], others[p], recv_a.at[p]).wait()
        synthesize(p, land, first_cat, cos_ref, sin_ref, high_ref, low_ref, made)
        for d in (2, 1, 3):
            copy = across(p, d)
            copy.start()
            sent.append(copy)
        forward(p, 0)

    def pass_on(p):
        for d in (1, 3, 2):
            forward(p, d)

    def finish_part(p):
        for wait in landed[p]:
            wait()
        for l in range(NLON):
            plain_ref[l, p // 2, pl.ds(p % 2, 64, stride=2), :] = ext[p][1, l, 4:68, :]
        lens(p, blk, src_ref, shift_ref, ext[p], toep, lensed_ref)

    turn(0)
    turn(1)
    pass_on(0)
    turn(2)
    pass_on(1)
    finish_part(0)
    turn(3)
    pass_on(2)
    finish_part(1)
    pass_on(3)
    finish_part(2)
    finish_part(3)
    for p in range(PARTS):
        pltpu.make_async_copy(others[p], others[p], send_a.at[p]).wait()
    for copy in sent:
        copy.wait_send()


def finish(plain_vmem, lensed_vmem, plain_ref, lensed_ref, sems):
    copies = [
        pltpu.make_async_copy(plain_vmem, plain_ref, sems.at[0]),
        pltpu.make_async_copy(lensed_vmem, lensed_ref, sems.at[1]),
    ]
    for copy in copies:
        copy.start()
    for copy in copies:
        copy.wait()


def shards(spectra, source_tiles, tap_shift, kernels):
    spec = spectra.reshape(NBLK, 2, 2, 2, 2, 128).transpose(0, 1, 2, 4, 3, 5)
    operands = (
        spec.reshape(NBLK, PARTS, 4, 128),
        source_tiles.transpose(0, 2, 1).reshape(2, 8),
        tap_shift.transpose(0, 2, 1).reshape(2, 8),
        kernels.reshape(16, 128),
        *map(jnp.asarray, tables()),
    )
    vmem = pl.BlockSpec(memory_space=pltpu.VMEM)
    hbm = pl.BlockSpec(memory_space=pltpu.HBM)
    dma = pltpu.SemaphoreType.DMA
    shape = jax.ShapeDtypeStruct((NLON, 2, 128, 128), F32)
    maps_in_vmem = pl.pallas_call(
        kernel,
        out_shape=(shape, shape),
        in_specs=[hbm] * 8,
        out_specs=(vmem, vmem),
        scratch_shapes=[pltpu.VMEM((3, NLON, ROWS, 128), F32)] * PARTS
        + [
            pltpu.VMEM((PARTS, NBLK, 4, 128), F32),
            pltpu.VMEM((PARTS, NLON, ROWS, 128), F32),
            pltpu.VMEM((8, 768, 256), BF16),
            pltpu.SMEM((2, 8), jnp.int32),
            pltpu.SMEM((2, 8), jnp.int32),
            pltpu.VMEM((32, 128), F32),
            pltpu.VMEM((512, 256), F32),
            pltpu.VMEM((128, 256), F32),
            pltpu.VMEM((128, 256), F32),
            pltpu.VMEM((NLON * ROWS, 512), F32),
            pltpu.VMEM((512, 768), BF16),
            pltpu.VMEM((NLON * ROWS, 512), BF16),
            pltpu.VMEM((NLON * ROWS, 512), BF16),
            dma((11 + PARTS,)),
            dma((PARTS,)),
            dma((PARTS,)),
            dma((PARTS, NLON)),
            dma((PARTS, NLON)),
            dma((PARTS, 2, NLON)),
            dma((PARTS, 2, NLON)),
        ],
        compiler_params=pltpu.CompilerParams(
            collective_id=0, has_side_effects=True, vmem_limit_bytes=32 * 1024 * 1024
        ),
    )(*(pltpu.with_memory_space_constraint(x, pltpu.HBM) for x in operands))
    plain, lensed = pl.pallas_call(
        finish,
        out_shape=(shape, shape),
        in_specs=[vmem, vmem],
        out_specs=(hbm, hbm),
        scratch_shapes=[dma((2,))],
        compiler_params=pltpu.CompilerParams(vmem_limit_bytes=16 * 1024 * 1024),
    )(*maps_in_vmem)

    def maps(x):
        return x.reshape(8, 64, 2, 128).transpose(0, 2, 1, 3).reshape(8, 2, 8192)

    return maps(plain), maps(lensed)


def solution(mesh):
    placed = (
        P(None, "lon", None, None, None, "blk"),
        P("blk", "lon", None),
        P("blk", "lon", None),
        P("blk", "lon", None, None),
    )
    return jax.shard_map(
        shards,
        mesh=mesh,
        in_specs=placed,
        out_specs=(P("blk", None, "lon"), P("blk", None, "lon")),
        check_vma=False,
    )
```

time: 45.2 us -> 41.1 us (0.909)
  Pallas kernels: 44 us -> 40 us
    pallas_call x2, Pallas kernels: 44 us -> 40 us  [the longest x1 39.1 us: shards(): pl.pallas_call(kernel, out_shape=(shape, shape), in_specs=[hbm] * 8, out_...]
where the time goes in v4:
time: 41.1 us; the launch traced here: 40.7 us
  Pallas kernels  40 us (97%)
  between operations  0.64 us (2%)
    pallas_call x1, Pallas kernels, shards(): pl.pallas_call(kernel, out_shape=(shape, shape), in_specs=[hbm] * 8, out_...  39.1 us
    pallas_call x1, Pallas kernels, shards(): pl.pallas_call(finish, out_shape=(shape, shape), in_specs=[vmem, vmem], o...  0.99 us

profile of v4, /device:TPU:1, one launch (start us, length us, event | category | flops | bytes accessed | tf_op | source)
XLA Modules:
  0.0 40.7 jit_solution(4324576331719671452)
XLA Ops:
  0.6 39.1 %shard_map.95 = (f32[4,2,128,128]{3,2,1,0:T(8,128)S(1)}, f32[4,2,128,128]{3,2,1,0:T(8,128)S(1)}) custom-call(f32[64,4,4,128]{3,2,1,0:T(4,128)} %bitcast.22, s32[2,8]{1,0:T(2,128)} %bitcast.24, s32[2,8]{1,0:T(2,128)} %bitcast.25, f32[16,128]{1,0:T(8,128)} %bitcast.23, f32[512,256]{1,0:T(8,128)} %constant.8.clone.first_hbm, f32[128,256]{1,0:T(8,128)} %constant.9.clone.cos_hbm, ...), custom_call_target="tpu_custom_call" | custom-call | tf_op jit(solution)/shard_map/pallas_call | solution.py:297
  39.7 1.0 %shard_map.96 = (f32[4,2,128,128]{3,2,1,0:T(8,128)}, f32[4,2,128,128]{3,2,1,0:T(8,128)}) custom-call(f32[4,2,128,128]{3,2,1,0:T(8,128)S(1)} %get-tuple-element.6.plain_vmem, f32[4,2,128,128]{3,2,1,0:T(8,128)S(1)} %get-tuple-element.7.lensed_vmem), custom_call_target="tpu_custom_call" | custom-call | tf_op jit(solution)/shard_map/pallas_call | solution.py:329

commit v5 on v4

--- a/solution.py
+++ b/solution.py
@@ -53,18 +53,19 @@
     return lax.dot_general(a, b, (((1,), (1,)), ((), ())), preferred_element_type=F32)
 
 
-def synthesize(p, land, first_ref, cos_ref, sin_ref, high_ref, low_ref, made):
-    xh, xl = halves(land[p].reshape(4 * NBLK, 128))
-    g = dot(first_ref[...], jnp.concatenate([xh, xh, xl], axis=0))
+def synthesize(p, land, first_ref, cos_ref, sin_ref, last_ref, made):
+    x = jnp.concatenate(halves(land[p].reshape(4 * NBLK, 128)), axis=1)
+    r = dot(first_ref[...], x)
+    g = r[:512, :128] + (r[:512, 128:] + r[512:, :128])
     real, imag = [], []
     for h in range(2):
         gre, gim = g[256 * h : 256 * h + 128], g[256 * h + 128 : 256 * h + 256]
         cos, sin = cos_ref[:, 128 * h : 128 * h + 128], sin_ref[:, 128 * h : 128 * h + 128]
         real.append(gre * cos - gim * sin)
         imag.append(gre * sin + gim * cos)
-    hh, hl = halves(jnp.concatenate(real + imag, axis=1))
-    out = nt(high_ref[...], hh) + (nt(low_ref[...], hh) + nt(high_ref[...], hl))
-    made[p] = out.reshape(NLON, ROWS, 128)
+    r = nt(last_ref[...], jnp.concatenate(halves(jnp.concatenate(real + imag, axis=1)), axis=0))
+    count = NLON * ROWS
+    made[p] = (r[:count, :128] + (r[:count, 128:] + r[count:, :128])).reshape(NLON, ROWS, 128)
 
 
 def base_of(shift):
@@ -124,7 +125,7 @@
     spec_ref, src_hbm, shift_hbm, taps_hbm, first_hbm, cos_hbm, sin_hbm, last_hbm,
     plain_ref, lensed_ref,
     ext_0, ext_1, ext_2, ext_3, land, made, toep, src_ref, shift_ref, taps_ref,
-    first_ref, cos_ref, sin_ref, last_ref, first_cat, high_ref, low_ref,
+    first_ref, cos_ref, sin_ref, last_ref, first_cat, last_cat,
     own_sem, send_a, recv_a, send_b, recv_b, send_c, recv_c,
 ):
     ext = (ext_0, ext_1, ext_2, ext_3)
@@ -132,6 +133,9 @@
     lon = lax.axis_index("lon")
     up = lax.rem(blk + 1, NBLK)
     down = lax.rem(blk + NBLK - 1, NBLK)
+    odd = lax.rem(blk, 2)
+    near = blk + 1 - 2 * odd
+    far = lax.rem(blk + NBLK - 1 + 2 * odd, NBLK)
 
     barrier = pltpu.get_barrier_semaphore()
 
@@ -141,11 +145,12 @@
         )
         return carry
 
-    lax.fori_loop(1, NBLK, greet, 0)
+    lax.fori_loop(1, NBLK, greet, 0, unroll=9)
     for d in range(1, NLON):
-        pl.semaphore_signal(
-            barrier, inc=1, device_id=(blk, lax.rem(lon + d, NLON)), device_id_type=MESH
-        )
+        for to in (blk, far):
+            pl.semaphore_signal(
+                barrier, inc=1, device_id=(to, lax.rem(lon + d, NLON)), device_id_type=MESH
+            )
     loads = [
         pltpu.make_async_copy(source, target, own_sem.at[j])
         for j, (source, target) in enumerate(
@@ -163,7 +168,7 @@
     ]
     for load in loads:
         load.start()
-    pl.semaphore_wait(barrier, NBLK - 1 + NLON - 1)
+    pl.semaphore_wait(barrier, NBLK - 1 + 2 * (NLON - 1))
 
     for p in range(PARTS):
 
@@ -179,15 +184,12 @@
             ).start()
             return carry
 
-        lax.fori_loop(1, NBLK, send, 0)
+        lax.fori_loop(1, NBLK, send, 0, unroll=3)
 
     for load in loads:
         load.wait()
-    fh, fl = halves(first_ref[...])
-    first_cat[...] = jnp.concatenate([fh, fl, fh], axis=1)
-    lh, ll = halves(last_ref[...])
-    high_ref[...] = lh
-    low_ref[...] = ll
+    first_cat[...] = jnp.concatenate(halves(first_ref[...]), axis=0)
+    last_cat[...] = jnp.concatenate(halves(last_ref[...]), axis=0)
     place_taps(shift_ref, taps_ref, toep)
 
     others = [land.at[p, pl.ds(0, NBLK - 1)] for p in range(PARTS)]
@@ -197,83 +199,91 @@
         return pltpu.make_async_remote_copy(
             src_ref=made.at[p, to],
             dst_ref=ext[p].at[1, lon],
-            send_sem=send_b.at[p, d],
+            send_sem=send_b,
             recv_sem=recv_b.at[p, d],
             device_id=(blk, to),
             device_id_type=MESH,
         )
 
-    def beside(p, d, source, to, slot, side):
-        l = lax.rem(lon + NLON - d, NLON)
-        return pltpu.make_async_remote_copy(
+    def beside(p, source, l, row, to, slot):
+        pltpu.make_async_remote_copy(
             src_ref=source,
             dst_ref=ext[p].at[slot, l],
-            send_sem=send_c.at[p, side, d],
-            recv_sem=recv_c.at[p, side, d],
-            device_id=(to, lon),
+            send_sem=send_c.at[p],
+            recv_sem=recv_c.at[p],
+            device_id=(row, to),
             device_id_type=MESH,
-        )
-
-    sent = []
-    landed = [[] for _ in range(PARTS)]
-
-    def forward(p, d):
+        ).start()
+
+    def keep(p):
+        return pltpu.make_async_copy(made.at[p, lon], ext[p].at[1, lon], own_sem.at[11 + p])
+
+    def pass_on(p, d):
+        l = lax.rem(lon + NLON - d, NLON)
         if d == 0:
             source = made.at[p, lon]
-            keep = pltpu.make_async_copy(source, ext[p].at[1, lon], own_sem.at[11 + p])
-            keep.start()
-            landed[p].append(keep.wait)
         else:
             across(p, d).wait_recv()
-            source = ext[p].at[1, lax.rem(lon + NLON - d, NLON)]
-        for to, slot, side in ((up, 0, 0), (down, 2, 1)):
-            copy = beside(p, d, source, to, slot, side)
-            copy.start()
-            sent.append(copy)
-            landed[p].append(copy.wait_recv)
+            source = ext[p].at[1, l]
+        if p < PARTS - 1:
+            beside(p, source, l, up, lon, 0)
+            beside(p, source, l, down, lon, 2)
+        else:
+            beside(p, source, l, near, lon, 2 * odd)
 
     def turn(p):
         pltpu.make_async_copy(others[p], others[p], recv_a.at[p]).wait()
-        synthesize(p, land, first_cat, cos_ref, sin_ref, high_ref, low_ref, made)
-        for d in (2, 1, 3):
-            copy = across(p, d)
-            copy.start()
-            sent.append(copy)
-        forward(p, 0)
-
-    def pass_on(p):
-        for d in (1, 3, 2):
-            forward(p, d)
+        synthesize(p, land, first_cat, cos_ref, sin_ref, last_cat, made)
+        for d in (2, 1, 3, 0):
+            to = lax.rem(lon + d, NLON)
+            if p == PARTS - 1:
+                beside(p, made.at[p, to], lon, far, to, 2 - 2 * odd)
+            if d != 0:
+                across(p, d).start()
+        pass_on(p, 0)
+        keep(p).start()
 
     def finish_part(p):
-        for wait in landed[p]:
-            wait()
+        rows = ext[p].at[pl.ds(0, 2)]
+        pltpu.make_async_copy(rows, rows, recv_c.at[p]).wait()
+        keep(p).wait()
         for l in range(NLON):
             plain_ref[l, p // 2, pl.ds(p % 2, 64, stride=2), :] = ext[p][1, l, 4:68, :]
         lens(p, blk, src_ref, shift_ref, ext[p], toep, lensed_ref)
 
+    def sent(p):
+        rows = ext[p].at[pl.ds(0, 2)]
+        pltpu.make_async_copy(rows, rows, send_c.at[p]).wait()
+        pltpu.make_async_copy(others[p], others[p], send_a.at[p]).wait()
+
     turn(0)
     turn(1)
-    pass_on(0)
+    for d in (1, 3, 2):
+        pass_on(0, d)
     turn(2)
-    pass_on(1)
+    for d in (1, 3, 2):
+        pass_on(1, d)
     finish_part(0)
     turn(3)
-    pass_on(2)
+    for d in (1, 3, 2):
+        pass_on(2, d)
     finish_part(1)
-    pass_on(3)
+    for d in (1, 3, 2):
+        pass_on(3, d)
     finish_part(2)
+    for p in range(3):
+        sent(p)
+    every = made.at[:, pl.ds(0, NLON - 1)]
+    pltpu.make_async_copy(every, every, send_b).wait()
     finish_part(3)
-    for p in range(PARTS):
-        pltpu.make_async_copy(others[p], others[p], send_a.at[p]).wait()
-    for copy in sent:
-        copy.wait_send()
+    sent(3)
 
 
 def finish(plain_vmem, lensed_vmem, plain_ref, lensed_ref, sems):
     copies = [
-        pltpu.make_async_copy(plain_vmem, plain_ref, sems.at[0]),
-        pltpu.make_async_copy(lensed_vmem, lensed_ref, sems.at[1]),
+        pltpu.make_async_copy(source.at[l], target.at[l], sems.at[j, l])
+        for j, (source, target) in enumerate(((plain_vmem, plain_ref), (lensed_vmem, lensed_ref)))
+        for l in range(NLON)
     ]
     for copy in copies:
         copy.start()
@@ -311,16 +321,15 @@
             pltpu.VMEM((128, 256), F32),
             pltpu.VMEM((128, 256), F32),
             pltpu.VMEM((NLON * ROWS, 512), F32),
-            pltpu.VMEM((512, 768), BF16),
-            pltpu.VMEM((NLON * ROWS, 512), BF16),
-            pltpu.VMEM((NLON * ROWS, 512), BF16),
+            pltpu.VMEM((1024, 256), BF16),
+            pltpu.VMEM((2 * NLON * ROWS, 512), BF16),
             dma((11 + PARTS,)),
             dma((PARTS,)),
             dma((PARTS,)),
+            dma,
             dma((PARTS, NLON)),
-            dma((PARTS, NLON)),
-            dma((PARTS, 2, NLON)),
-            dma((PARTS, 2, NLON)),
+            dma((PARTS,)),
+            dma((PARTS,)),
         ],
         compiler_params=pltpu.CompilerParams(
             collective_id=0, has_side_effects=True, vmem_limit_bytes=32 * 1024 * 1024
@@ -331,7 +340,7 @@
         out_shape=(shape, shape),
         in_specs=[vmem, vmem],
         out_specs=(hbm, hbm),
-        scratch_shapes=[dma((2,))],
+        scratch_shapes=[dma((2, NLON))],
         compiler_params=pltpu.CompilerParams(vmem_limit_bytes=16 * 1024 * 1024),
     )(*maps_in_vmem)
 

time: 41.1 us -> 39.8 us (0.968)
  Pallas kernels: 40 us -> 39 us
    pallas_call x1, Pallas kernels: 39.1 us -> 38 us  [shards(): pl.pallas_call(kernel, out_shape=(shape, shape), in_specs=[hbm] * 8, out_...]
where the time goes in v5:
time: 39.8 us; the launch traced here: 39.6 us
  Pallas kernels  39 us (98%)
  between operations  0.64 us (2%)
    pallas_call x1, Pallas kernels, shards(): pl.pallas_call(kernel, out_shape=(shape, shape), in_specs=[hbm] * 8, out_...  38 us
    pallas_call x1, Pallas kernels, shards(): pl.pallas_call(finish, out_shape=(shape, shape), in_specs=[vmem, vmem], o...  1.03 us

profile of v5, /device:TPU:1, one launch (start us, length us, event | category | flops | bytes accessed | tf_op | source)
XLA Modules:
  0.0 39.6 jit_solution(9352858520225827780)
XLA Ops:
  0.6 38.0 %shard_map.95 = (f32[4,2,128,128]{3,2,1,0:T(8,128)S(1)}, f32[4,2,128,128]{3,2,1,0:T(8,128)S(1)}) custom-call(f32[64,4,4,128]{3,2,1,0:T(4,128)} %bitcast.22, s32[2,8]{1,0:T(2,128)} %bitcast.24, s32[2,8]{1,0:T(2,128)} %bitcast.25, f32[16,128]{1,0:T(8,128)} %bitcast.23, f32[512,256]{1,0:T(8,128)} %constant.8.clone.first_hbm, f32[128,256]{1,0:T(8,128)} %constant.9.clone.cos_hbm, ...), custom_call_target="tpu_custom_call" | custom-call | tf_op jit(solution)/shard_map/pallas_call | solution.py:307
  38.6 1.0 %shard_map.96 = (f32[4,2,128,128]{3,2,1,0:T(8,128)}, f32[4,2,128,128]{3,2,1,0:T(8,128)}) custom-call(f32[4,2,128,128]{3,2,1,0:T(8,128)S(1)} %get-tuple-element.6.plain_vmem, f32[4,2,128,128]{3,2,1,0:T(8,128)S(1)} %get-tuple-element.7.lensed_vmem), custom_call_target="tpu_custom_call" | custom-call | tf_op jit(solution)/shard_map/pallas_call | solution.py:338

commit v6 on v5

--- a/solution.py
+++ b/solution.py
@@ -11,6 +11,7 @@
 NBLK = 64
 NLON = 4
 PARTS = 4
+DIRECT = 2
 MESH = pl.DeviceIdType.MESH
 F32 = jnp.float32
 BF16 = jnp.bfloat16
@@ -53,7 +54,7 @@
     return lax.dot_general(a, b, (((1,), (1,)), ((), ())), preferred_element_type=F32)
 
 
-def synthesize(p, land, first_ref, cos_ref, sin_ref, last_ref, made):
+def transform(p, land, first_ref, cos_ref, sin_ref):
     x = jnp.concatenate(halves(land[p].reshape(4 * NBLK, 128)), axis=1)
     r = dot(first_ref[...], x)
     g = r[:512, :128] + (r[:512, 128:] + r[512:, :128])
@@ -63,9 +64,12 @@
         cos, sin = cos_ref[:, 128 * h : 128 * h + 128], sin_ref[:, 128 * h : 128 * h + 128]
         real.append(gre * cos - gim * sin)
         imag.append(gre * sin + gim * cos)
-    r = nt(last_ref[...], jnp.concatenate(halves(jnp.concatenate(real + imag, axis=1)), axis=0))
-    count = NLON * ROWS
-    made[p] = (r[:count, :128] + (r[:count, 128:] + r[count:, :128])).reshape(NLON, ROWS, 128)
+    return jnp.concatenate(halves(jnp.concatenate(real + imag, axis=1)), axis=0)
+
+
+def pixels(last_ref, l, turned):
+    r = nt(last_ref[pl.ds(pl.multiple_of(2 * ROWS * l, 16), 2 * ROWS), :], turned)
+    return r[:ROWS, :128] + (r[:ROWS, 128:] + r[ROWS:, :128])
 
 
 def base_of(shift):
@@ -131,11 +135,10 @@
     ext = (ext_0, ext_1, ext_2, ext_3)
     blk = lax.axis_index("blk")
     lon = lax.axis_index("lon")
-    up = lax.rem(blk + 1, NBLK)
-    down = lax.rem(blk + NBLK - 1, NBLK)
     odd = lax.rem(blk, 2)
     near = blk + 1 - 2 * odd
-    far = lax.rem(blk + NBLK - 1 + 2 * odd, NBLK)
+    far = blk - 1 + 2 * odd
+    has_far = (blk > 0) & (blk < NBLK - 1)
 
     barrier = pltpu.get_barrier_semaphore()
 
@@ -147,10 +150,17 @@
 
     lax.fori_loop(1, NBLK, greet, 0, unroll=9)
     for d in range(1, NLON):
-        for to in (blk, far):
+        pl.semaphore_signal(
+            barrier, inc=1, device_id=(blk, lax.rem(lon + d, NLON)), device_id_type=MESH
+        )
+
+    @pl.when(has_far)
+    def _():
+        for d in range(1, NLON):
             pl.semaphore_signal(
-                barrier, inc=1, device_id=(to, lax.rem(lon + d, NLON)), device_id_type=MESH
+                barrier, inc=1, device_id=(far, lax.rem(lon + d, NLON)), device_id_type=MESH
             )
+
     loads = [
         pltpu.make_async_copy(source, target, own_sem.at[j])
         for j, (source, target) in enumerate(
@@ -168,28 +178,37 @@
     ]
     for load in loads:
         load.start()
-    pl.semaphore_wait(barrier, NBLK - 1 + 2 * (NLON - 1))
+    pl.semaphore_wait(
+        barrier, NBLK - 1 + (NLON - 1) * (1 + has_far.astype(jnp.int32))
+    )
 
     for p in range(PARTS):
 
         def send(o, carry, p=p):
-            to = lax.rem(blk + o, NBLK)
-            pltpu.make_async_remote_copy(
-                src_ref=spec_ref.at[to, p],
-                dst_ref=land.at[p, blk],
-                send_sem=send_a.at[p],
-                recv_sem=recv_a.at[p],
-                device_id=(to, lon),
-                device_id_type=MESH,
-            ).start()
+            to = 8 * (o // 8) + lax.rem(blk + o, 8)
+
+            @pl.when(to != blk)
+            def _():
+                pltpu.make_async_remote_copy(
+                    src_ref=spec_ref.at[to, p],
+                    dst_ref=land.at[p, blk],
+                    send_sem=send_a.at[p],
+                    recv_sem=recv_a.at[p],
+                    device_id=(to, lon),
+                    device_id_type=MESH,
+                ).start()
+
             return carry
 
-        lax.fori_loop(1, NBLK, send, 0, unroll=3)
+        lax.fori_loop(0, NBLK, send, 0)
 
     for load in loads:
         load.wait()
     first_cat[...] = jnp.concatenate(halves(first_ref[...]), axis=0)
-    last_cat[...] = jnp.concatenate(halves(last_ref[...]), axis=0)
+    for l in range(NLON):
+        last_cat[2 * ROWS * l : 2 * ROWS * (l + 1)] = jnp.concatenate(
+            halves(last_ref[ROWS * l : ROWS * (l + 1)]), axis=0
+        )
     place_taps(shift_ref, taps_ref, toep)
 
     others = [land.at[p, pl.ds(0, NBLK - 1)] for p in range(PARTS)]
@@ -205,74 +224,84 @@
             device_id_type=MESH,
         )
 
-    def beside(p, source, l, row, to, slot):
+    def beside(p, source, l, row, to, slot, side):
         pltpu.make_async_remote_copy(
             src_ref=source,
             dst_ref=ext[p].at[slot, l],
-            send_sem=send_c.at[p],
-            recv_sem=recv_c.at[p],
+            send_sem=send_c.at[side, p],
+            recv_sem=recv_c.at[side, p],
             device_id=(row, to),
             device_id_type=MESH,
         ).start()
 
+    def to_near(p, source, l):
+        beside(p, source, l, near, lon, 2 * odd, 0)
+
+    def to_far(p, source, l, to):
+        @pl.when(has_far)
+        def _():
+            beside(p, source, l, far, to, 2 - 2 * odd, 1)
+
     def keep(p):
         return pltpu.make_async_copy(made.at[p, lon], ext[p].at[1, lon], own_sem.at[11 + p])
 
-    def pass_on(p, d):
-        l = lax.rem(lon + NLON - d, NLON)
-        if d == 0:
-            source = made.at[p, lon]
-        else:
-            across(p, d).wait_recv()
-            source = ext[p].at[1, l]
-        if p < PARTS - 1:
-            beside(p, source, l, up, lon, 0)
-            beside(p, source, l, down, lon, 2)
-        else:
-            beside(p, source, l, near, lon, 2 * odd)
-
     def turn(p):
         pltpu.make_async_copy(others[p], others[p], recv_a.at[p]).wait()
-        synthesize(p, land, first_cat, cos_ref, sin_ref, last_cat, made)
+        turned = transform(p, land, first_cat, cos_ref, sin_ref)
         for d in (2, 1, 3, 0):
             to = lax.rem(lon + d, NLON)
-            if p == PARTS - 1:
-                beside(p, made.at[p, to], lon, far, to, 2 - 2 * odd)
+            made[p, to] = pixels(last_cat, to, turned)
             if d != 0:
                 across(p, d).start()
-        pass_on(p, 0)
+            if d == 0 or p >= DIRECT:
+                to_far(p, made.at[p, to], lon, to)
+        to_near(p, made.at[p, lon], lon)
         keep(p).start()
 
+    def pass_on(p):
+        for d in (1, 3, 2):
+            l = lax.rem(lon + NLON - d, NLON)
+            across(p, d).wait_recv()
+            to_near(p, ext[p].at[1, l], l)
+            if p < DIRECT:
+                to_far(p, ext[p].at[1, l], l, lon)
+
     def finish_part(p):
-        rows = ext[p].at[pl.ds(0, 2)]
-        pltpu.make_async_copy(rows, rows, recv_c.at[p]).wait()
         keep(p).wait()
         for l in range(NLON):
             plain_ref[l, p // 2, pl.ds(p % 2, 64, stride=2), :] = ext[p][1, l, 4:68, :]
+        rows = ext[p].at[0]
+        pltpu.make_async_copy(rows, rows, recv_c.at[0, p]).wait()
+
+        @pl.when(has_far)
+        def _():
+            pltpu.make_async_copy(rows, rows, recv_c.at[1, p]).wait()
+
         lens(p, blk, src_ref, shift_ref, ext[p], toep, lensed_ref)
 
     def sent(p):
-        rows = ext[p].at[pl.ds(0, 2)]
-        pltpu.make_async_copy(rows, rows, send_c.at[p]).wait()
+        rows = ext[p].at[0]
+        pltpu.make_async_copy(rows, rows, send_c.at[0, p]).wait()
+
+        @pl.when(has_far)
+        def _():
+            pltpu.make_async_copy(rows, rows, send_c.at[1, p]).wait()
+
         pltpu.make_async_copy(others[p], others[p], send_a.at[p]).wait()
 
     turn(0)
     turn(1)
-    for d in (1, 3, 2):
-        pass_on(0, d)
+    pass_on(0)
     turn(2)
-    for d in (1, 3, 2):
-        pass_on(1, d)
+    pass_on(1)
     finish_part(0)
     turn(3)
-    for d in (1, 3, 2):
-        pass_on(2, d)
+    pass_on(2)
     finish_part(1)
-    for d in (1, 3, 2):
-        pass_on(3, d)
-    finish_part(2)
+    pass_on(3)
     for p in range(3):
         sent(p)
+    finish_part(2)
     every = made.at[:, pl.ds(0, NLON - 1)]
     pltpu.make_async_copy(every, every, send_b).wait()
     finish_part(3)
@@ -328,8 +357,8 @@
             dma((PARTS,)),
             dma,
             dma((PARTS, NLON)),
-            dma((PARTS,)),
-            dma((PARTS,)),
+            dma((2, PARTS)),
+            dma((2, PARTS)),
         ],
         compiler_params=pltpu.CompilerParams(
             collective_id=0, has_side_effects=True, vmem_limit_bytes=32 * 1024 * 1024

time: 39.8 us -> 37.3 us (0.937)
  the two profiles are of different devices: /device:TPU:1 before, /device:TPU:33 now
where the time goes in v6:
time: 37.3 us; the launch traced here: 37.2 us
  Pallas kernels  36.6 us (98%)
  between operations  0.64 us (2%)
    pallas_call x1, Pallas kernels, shards(): pl.pallas_call(kernel, out_shape=(shape, shape), in_specs=[hbm] * 8, out_...  35.6 us
    pallas_call x1, Pallas kernels, shards(): pl.pallas_call(finish, out_shape=(shape, shape), in_specs=[vmem, vmem], o...  1.03 us

profile of v6, /device:TPU:33, one launch (start us, length us, event | category | flops | bytes accessed | tf_op | source)
XLA Modules:
  0.0 37.2 jit_solution(2707776191444627287)
XLA Ops:
  0.6 35.6 %shard_map.95 = (f32[4,2,128,128]{3,2,1,0:T(8,128)S(1)}, f32[4,2,128,128]{3,2,1,0:T(8,128)S(1)}) custom-call(f32[64,4,4,128]{3,2,1,0:T(4,128)} %bitcast.22, s32[2,8]{1,0:T(2,128)} %bitcast.24, s32[2,8]{1,0:T(2,128)} %bitcast.25, f32[16,128]{1,0:T(8,128)} %bitcast.23, f32[512,256]{1,0:T(8,128)} %constant.8.clone.first_hbm, f32[128,256]{1,0:T(8,128)} %constant.9.clone.cos_hbm, ...), custom_call_target="tpu_custom_call" | custom-call | tf_op jit(solution)/shard_map/pallas_call | solution.py:336
  36.2 1.0 %shard_map.96 = (f32[4,2,128,128]{3,2,1,0:T(8,128)}, f32[4,2,128,128]{3,2,1,0:T(8,128)}) custom-call(f32[4,2,128,128]{3,2,1,0:T(8,128)S(1)} %get-tuple-element.6.plain_vmem, f32[4,2,128,128]{3,2,1,0:T(8,128)S(1)} %get-tuple-element.7.lensed_vmem), custom_call_target="tpu_custom_call" | custom-call | tf_op jit(solution)/shard_map/pallas_call | solution.py:367

commit v7 on v6

--- a/solution.py
+++ b/solution.py
@@ -248,7 +248,7 @@
     def turn(p):
         pltpu.make_async_copy(others[p], others[p], recv_a.at[p]).wait()
         turned = transform(p, land, first_cat, cos_ref, sin_ref)
-        for d in (2, 1, 3, 0):
+        for d in (1, 3, 2, 0):
             to = lax.rem(lon + d, NLON)
             made[p, to] = pixels(last_cat, to, turned)
             if d != 0:
@@ -294,14 +294,14 @@
     pass_on(0)
     turn(2)
     pass_on(1)
+    turn(3)
     finish_part(0)
-    turn(3)
     pass_on(2)
     finish_part(1)
     pass_on(3)
+    finish_part(2)
     for p in range(3):
         sent(p)
-    finish_part(2)
     every = made.at[:, pl.ds(0, NLON - 1)]
     pltpu.make_async_copy(every, every, send_b).wait()
     finish_part(3)

time: 37.3 us -> 36.2 us (0.971)
  the two profiles are of different devices: /device:TPU:33 before, /device:TPU:1 now
where the time goes in v7:
time: 36.2 us; the launch traced here: 36.1 us
  Pallas kernels  35.4 us (98%)
  between operations  0.64 us (2%)
    pallas_call x1, Pallas kernels, shards(): pl.pallas_call(kernel, out_shape=(shape, shape), in_specs=[hbm] * 8, out_...  34.4 us
    pallas_call x1, Pallas kernels, shards(): pl.pallas_call(finish, out_shape=(shape, shape), in_specs=[vmem, vmem], o...  1.03 us

profile of v7, /device:TPU:1, one launch (start us, length us, event | category | flops | bytes accessed | tf_op | source)
XLA Modules:
  0.0 36.1 jit_solution(4828137968994123649)
XLA Ops:
  0.6 34.4 %shard_map.95 = (f32[4,2,128,128]{3,2,1,0:T(8,128)S(1)}, f32[4,2,128,128]{3,2,1,0:T(8,128)S(1)}) custom-call(f32[64,4,4,128]{3,2,1,0:T(4,128)} %bitcast.22, s32[2,8]{1,0:T(2,128)} %bitcast.24, s32[2,8]{1,0:T(2,128)} %bitcast.25, f32[16,128]{1,0:T(8,128)} %bitcast.23, f32[512,256]{1,0:T(8,128)} %constant.8.clone.first_hbm, f32[128,256]{1,0:T(8,128)} %constant.9.clone.cos_hbm, ...), custom_call_target="tpu_custom_call" | custom-call | tf_op jit(solution)/shard_map/pallas_call | solution.py:336
  35.0 1.0 %shard_map.96 = (f32[4,2,128,128]{3,2,1,0:T(8,128)}, f32[4,2,128,128]{3,2,1,0:T(8,128)}) custom-call(f32[4,2,128,128]{3,2,1,0:T(8,128)S(1)} %get-tuple-element.6.plain_vmem, f32[4,2,128,128]{3,2,1,0:T(8,128)S(1)} %get-tuple-element.7.lensed_vmem), custom_call_target="tpu_custom_call" | custom-call | tf_op jit(solution)/shard_map/pallas_call | solution.py:367

commit v8 on v7

--- a/solution.py
+++ b/solution.py
@@ -182,34 +182,36 @@
         barrier, NBLK - 1 + (NLON - 1) * (1 + has_far.astype(jnp.int32))
     )
 
-    for p in range(PARTS):
-
-        def send(o, carry, p=p):
-            to = 8 * (o // 8) + lax.rem(blk + o, 8)
-
-            @pl.when(to != blk)
+    def send_spectra(p):
+        def one(to):
+            pltpu.make_async_remote_copy(
+                src_ref=spec_ref.at[to, p],
+                dst_ref=land.at[p, blk],
+                send_sem=send_a.at[p],
+                recv_sem=recv_a.at[p],
+                device_id=(to, lon),
+                device_id_type=MESH,
+            ).start()
+
+        def send(plane, carry):
+            @pl.when(plane != blk // 8)
             def _():
-                pltpu.make_async_remote_copy(
-                    src_ref=spec_ref.at[to, p],
-                    dst_ref=land.at[p, blk],
-                    send_sem=send_a.at[p],
-                    recv_sem=recv_a.at[p],
-                    device_id=(to, lon),
-                    device_id_type=MESH,
-                ).start()
-
+                one(8 * plane + lax.rem(blk, 8))
+
+            for step in range(1, 8):
+                one(8 * plane + lax.rem(blk + step, 8))
             return carry
 
-        lax.fori_loop(0, NBLK, send, 0)
-
-    for load in loads:
-        load.wait()
-    first_cat[...] = jnp.concatenate(halves(first_ref[...]), axis=0)
-    for l in range(NLON):
-        last_cat[2 * ROWS * l : 2 * ROWS * (l + 1)] = jnp.concatenate(
-            halves(last_ref[ROWS * l : ROWS * (l + 1)]), axis=0
-        )
-    place_taps(shift_ref, taps_ref, toep)
+        lax.fori_loop(0, NBLK // 8, send, 0)
+
+    def prepare():
+        for load in loads:
+            load.wait()
+        first_cat[...] = jnp.concatenate(halves(first_ref[...]), axis=0)
+        for l in range(NLON):
+            last_cat[2 * ROWS * l : 2 * ROWS * (l + 1)] = jnp.concatenate(
+                halves(last_ref[ROWS * l : ROWS * (l + 1)]), axis=0
+            )
 
     others = [land.at[p, pl.ds(0, NBLK - 1)] for p in range(PARTS)]
 
@@ -289,6 +291,10 @@
 
         pltpu.make_async_copy(others[p], others[p], send_a.at[p]).wait()
 
+    for p in range(PARTS):
+        send_spectra(p)
+    prepare()
+    place_taps(shift_ref, taps_ref, toep)
     turn(0)
     turn(1)
     pass_on(0)

time: 36.2 us -> 36 us (level)
  no operation moved by 1% of the time
where the time goes in v8:
time: 36 us; the launch traced here: 35.9 us
  Pallas kernels  35.2 us (98%)
  between operations  0.64 us (2%)
    pallas_call x1, Pallas kernels, shards(): pl.pallas_call(kernel, out_shape=(shape, shape), in_specs=[hbm] * 8, out_...  34.2 us
    pallas_call x1, Pallas kernels, shards(): pl.pallas_call(finish, out_shape=(shape, shape), in_specs=[vmem, vmem], o...  1.03 us

profile of v8, /device:TPU:1, one launch (start us, length us, event | category | flops | bytes accessed | tf_op | source)
XLA Modules:
  0.0 35.9 jit_solution(15174660436707688586)
XLA Ops:
  0.6 34.2 %shard_map.95 = (f32[4,2,128,128]{3,2,1,0:T(8,128)S(1)}, f32[4,2,128,128]{3,2,1,0:T(8,128)S(1)}) custom-call(f32[64,4,4,128]{3,2,1,0:T(4,128)} %bitcast.22, s32[2,8]{1,0:T(2,128)} %bitcast.24, s32[2,8]{1,0:T(2,128)} %bitcast.25, f32[16,128]{1,0:T(8,128)} %bitcast.23, f32[512,256]{1,0:T(8,128)} %constant.8.clone.first_hbm, f32[128,256]{1,0:T(8,128)} %constant.9.clone.cos_hbm, ...), custom_call_target="tpu_custom_call" | custom-call | tf_op jit(solution)/shard_map/pallas_call | solution.py:342
  34.9 1.0 %shard_map.96 = (f32[4,2,128,128]{3,2,1,0:T(8,128)}, f32[4,2,128,128]{3,2,1,0:T(8,128)}) custom-call(f32[4,2,128,128]{3,2,1,0:T(8,128)S(1)} %get-tuple-element.6.plain_vmem, f32[4,2,128,128]{3,2,1,0:T(8,128)S(1)} %get-tuple-element.7.lensed_vmem), custom_call_target="tpu_custom_call" | custom-call | tf_op jit(solution)/shard_map/pallas_call | solution.py:373

commit v9 on v7

--- a/solution.py
+++ b/solution.py
@@ -178,6 +178,17 @@
     ]
     for load in loads:
         load.start()
+    def prepare():
+        for load in loads:
+            load.wait()
+        first_cat[...] = jnp.concatenate(halves(first_ref[...]), axis=0)
+        for l in range(NLON):
+            last_cat[2 * ROWS * l : 2 * ROWS * (l + 1)] = jnp.concatenate(
+                halves(last_ref[ROWS * l : ROWS * (l + 1)]), axis=0
+            )
+        place_taps(shift_ref, taps_ref, toep)
+
+    pl.when(blk < NBLK // 2)(prepare)
     pl.semaphore_wait(
         barrier, NBLK - 1 + (NLON - 1) * (1 + has_far.astype(jnp.int32))
     )
@@ -202,14 +213,7 @@
 
         lax.fori_loop(0, NBLK, send, 0)
 
-    for load in loads:
-        load.wait()
-    first_cat[...] = jnp.concatenate(halves(first_ref[...]), axis=0)
-    for l in range(NLON):
-        last_cat[2 * ROWS * l : 2 * ROWS * (l + 1)] = jnp.concatenate(
-            halves(last_ref[ROWS * l : ROWS * (l + 1)]), axis=0
-        )
-    place_taps(shift_ref, taps_ref, toep)
+    pl.when(blk >= NBLK // 2)(prepare)
 
     others = [land.at[p, pl.ds(0, NBLK - 1)] for p in range(PARTS)]
 

time: 36.2 us -> 36.1 us (level)
  no operation moved by 1% of the time
where the time goes in v9:
time: 36.1 us; the launch traced here: 36 us
  Pallas kernels  35.3 us (98%)
  between operations  0.64 us (2%)
    pallas_call x1, Pallas kernels, shards(): pl.pallas_call(kernel, out_shape=(shape, shape), in_specs=[hbm] * 8, out_...  34.3 us
    pallas_call x1, Pallas kernels, shards(): pl.pallas_call(finish, out_shape=(shape, shape), in_specs=[vmem, vmem], o...  1.03 us

profile of v9, /device:TPU:1, one launch (start us, length us, event | category | flops | bytes accessed | tf_op | source)
XLA Modules:
  0.0 36.0 jit_solution(11220917817913387891)
XLA Ops:
  0.6 34.3 %shard_map.95 = (f32[4,2,128,128]{3,2,1,0:T(8,128)S(1)}, f32[4,2,128,128]{3,2,1,0:T(8,128)S(1)}) custom-call(f32[64,4,4,128]{3,2,1,0:T(4,128)} %bitcast.22, s32[2,8]{1,0:T(2,128)} %bitcast.24, s32[2,8]{1,0:T(2,128)} %bitcast.25, f32[16,128]{1,0:T(8,128)} %bitcast.23, f32[512,256]{1,0:T(8,128)} %constant.8.clone.first_hbm, f32[128,256]{1,0:T(8,128)} %constant.9.clone.cos_hbm, ...), custom_call_target="tpu_custom_call" | custom-call | tf_op jit(solution)/shard_map/pallas_call | solution.py:340
  34.9 1.0 %shard_map.96 = (f32[4,2,128,128]{3,2,1,0:T(8,128)}, f32[4,2,128,128]{3,2,1,0:T(8,128)}) custom-call(f32[4,2,128,128]{3,2,1,0:T(8,128)S(1)} %get-tuple-element.6.plain_vmem, f32[4,2,128,128]{3,2,1,0:T(8,128)S(1)} %get-tuple-element.7.lensed_vmem), custom_call_target="tpu_custom_call" | custom-call | tf_op jit(solution)/shard_map/pallas_call | solution.py:371

commit v10 on v8

--- a/solution.py
+++ b/solution.py
@@ -302,8 +302,8 @@
     pass_on(1)
     turn(3)
     finish_part(0)
+    finish_part(1)
     pass_on(2)
-    finish_part(1)
     pass_on(3)
     finish_part(2)
     for p in range(3):

time: 36 us -> 36 us (level)
  no operation moved by 1% of the time
where the time goes in v10:
time: 36 us; the launch traced here: 35.9 us
  Pallas kernels  35.2 us (98%)
  between operations  0.64 us (2%)
    pallas_call x1, Pallas kernels, shards(): pl.pallas_call(kernel, out_shape=(shape, shape), in_specs=[hbm] * 8, out_...  34.2 us
    pallas_call x1, Pallas kernels, shards(): pl.pallas_call(finish, out_shape=(shape, shape), in_specs=[vmem, vmem], o...  1.03 us

profile of v10, /device:TPU:1, one launch (start us, length us, event | category | flops | bytes accessed | tf_op | source)
XLA Modules:
  0.0 35.9 jit_solution(2774464585986192133)
XLA Ops:
  0.6 34.2 %shard_map.95 = (f32[4,2,128,128]{3,2,1,0:T(8,128)S(1)}, f32[4,2,128,128]{3,2,1,0:T(8,128)S(1)}) custom-call(f32[64,4,4,128]{3,2,1,0:T(4,128)} %bitcast.22, s32[2,8]{1,0:T(2,128)} %bitcast.24, s32[2,8]{1,0:T(2,128)} %bitcast.25, f32[16,128]{1,0:T(8,128)} %bitcast.23, f32[512,256]{1,0:T(8,128)} %constant.8.clone.first_hbm, f32[128,256]{1,0:T(8,128)} %constant.9.clone.cos_hbm, ...), custom_call_target="tpu_custom_call" | custom-call | tf_op jit(solution)/shard_map/pallas_call | solution.py:342
  34.9 1.0 %shard_map.96 = (f32[4,2,128,128]{3,2,1,0:T(8,128)}, f32[4,2,128,128]{3,2,1,0:T(8,128)}) custom-call(f32[4,2,128,128]{3,2,1,0:T(8,128)S(1)} %get-tuple-element.6.plain_vmem, f32[4,2,128,128]{3,2,1,0:T(8,128)S(1)} %get-tuple-element.7.lensed_vmem), custom_call_target="tpu_custom_call" | custom-call | tf_op jit(solution)/shard_map/pallas_call | solution.py:373
